TPU v7x, 256 devices: a whole 4x4x8 slice. The times are simulated.
256 devices in a mesh: tm: 16 (over z_hi, y, core), tile: 16 (over z_lo, x).
Axes of the slice: x: 4, y: 4, z: 8 (z_hi: 2, z_lo: 4; z = z_hi * 4 + z_lo), core: 2. Of those that a mesh axis runs over, the one named last changes fastest.
Arguments:
- clip_tokens: bfloat16 [128, 16, 7, 7, 128], P('tm', 'tile'), may hold values from -6 to 6
- target: bfloat16 [128, 16, 7, 7, 128], P('tm', 'tile'), may hold values from -6 to 6
- norm1_gain: float32 [128], replicated, may hold values from 0.1 to 1.9
- norm1_bias: float32 [128], replicated, may hold values from -3 to 3
- qkv_weight: bfloat16 [128, 384], replicated, may hold values from -0.5 to 0.5
- qkv_bias: float32 [384], replicated, may hold values from -3 to 3
- bias_table: float32 [2535, 4], replicated, may hold values from -250 to 250
- proj_weight: bfloat16 [128, 128], replicated, may hold values from -0.5 to 0.5
- proj_bias: float32 [128], replicated, may hold values from -3 to 3
- norm2_gain: float32 [128], replicated, may hold values from 0.1 to 1.9
- norm2_bias: float32 [128], replicated, may hold values from -3 to 3
- fc1_weight: bfloat16 [128, 512], replicated, may hold values from -0.5 to 0.5
- fc1_bias: float32 [512], replicated, may hold values from -3 to 3
- fc2_weight: bfloat16 [512, 128], replicated, may hold values from -0.25 to 0.25
- fc2_bias: float32 [128], replicated, may hold values from -3 to 3
Outputs:
- grad_clip: bfloat16 [128, 16, 7, 7, 128], P('tm', 'tile')
All inputs are finite; a program needn't handle non-finite values.
Results may differ from a plain program's by a relative error of at most 0.0085.
Values may be sent and summed in bfloat16 or wider, within the bound.
A program may use at most 192 MiB of HBM per device.

v0:
```python
import itertools

import jax
import jax.numpy as jnp
import numpy as np
from jax import lax
from jax.experimental import pallas as pl
from jax.experimental.pallas import tpu as pltpu
from jax.sharding import PartitionSpec as P

HEADS = 4
HEAD = 32
CHAN = 128
FF = 512
WT = 8
WH = 7
WW = 7
ST = 4
SH = 3
SW = 3
TCOLS = 4
TROWS = 4
TM = 16
TOK = WT * WH * WW
KEYS = 512
SLAB = WW * WT

EPSILON = 1e-05
MASKED = -1000000000.0
ROOT_HALF = 0.7071067811865476
INV_ROOT_TAU = 0.3989422804014327
SCALE = HEAD ** (-0.5)

F32 = jnp.float32
BF16 = jnp.bfloat16
MESH = pl.DeviceIdType.MESH


def message_plan():
    parts_time = (range(ST, WT), range(0, ST))
    parts_rows = (range(SH, WH), range(0, SH))
    parts_cols = (range(SW, WW), range(0, SW))
    plan = []
    offset = 0
    for et, er, ec in itertools.product(range(2), range(2), range(2)):
        tile_rows = []
        window_rows = []
        for h, w, t in itertools.product(parts_rows[er], parts_cols[ec], parts_time[et]):
            tile_rows.append((h * WW + w) * WT + t)
            a, b, c = (t - ST) % WT, (h - SH) % WH, (w - SW) % WW
            window_rows.append((b * WW + c) * WT + a)
        size = -(-len(tile_rows) // 16) * 16
        plan.append(((et, er, ec), offset, size, tile_rows, window_rows))
        offset += size
    return plan, offset


PLAN, PACKED = message_plan()
AWAY = [cut for cut in PLAN if any(cut[0])]


def selectors():
    from_tile = np.zeros((PACKED, TOK), np.float32)
    from_window = np.zeros((PACKED, TOK), np.float32)
    for _, offset, _, tile_rows, window_rows in PLAN:
        for i, (tile_row, window_row) in enumerate(zip(tile_rows, window_rows)):
            from_tile[offset + i, tile_row] = 1.0
            from_window[offset + i, window_row] = 1.0
    return from_tile, from_window


def dot(a, b, dims=((1,), (0,))):
    return lax.dot_general(a, b, (dims, ((), ())), preferred_element_type=F32)


NT = ((1,), (1,))


def row_mean(values):
    return jnp.sum(values, -1, keepdims=True) * (1.0 / CHAN)


def norm_stats(values):
    center = values - row_mean(values)
    inv_std = lax.rsqrt(row_mean(center * center) + EPSILON)
    return center * inv_std, inv_std


def norm_backward(grad_out, normal, inv_std, gain):
    scaled = grad_out * gain
    return inv_std * (scaled - row_mean(scaled) - normal * row_mean(scaled * normal))


def iota(shape, dim):
    return lax.broadcasted_iota(jnp.int32, shape, dim)


def neighbour(sign, cut):
    time_pos = lax.axis_index("tm")
    tile_pos = lax.axis_index("tile")
    row, col = tile_pos // TCOLS, tile_pos % TCOLS
    et, er, ec = cut
    to_time = (time_pos + TM + sign * et) % TM
    to_row = (row + TROWS + sign * er) % TROWS
    to_col = (col + TCOLS + sign * ec) % TCOLS
    return {"tm": to_time, "tile": to_row * TCOLS + to_col}


def copies(src, dst, send_sems, recv_sems, sign):
    return [
        pltpu.make_async_remote_copy(
            src_ref=src.at[pl.ds(offset, size), :],
            dst_ref=dst.at[pl.ds(offset, size), :],
            send_sem=send_sems.at[i],
            recv_sem=recv_sems.at[i],
            device_id=neighbour(sign, cut),
            device_id_type=MESH,
        )
        for i, (cut, offset, size, _, _) in enumerate(AWAY)
    ]


def fill_bias(table, slab_ref, spread_ref, skew_ref, bias_ref):
    time_span, row_span, col_span = 2 * WT - 1, 2 * WH - 1, 2 * WW - 1
    plane = row_span * col_span
    for d in range(time_span):
        slab_ref[HEADS * d : HEADS * (d + 1), :] = table[:, d * plane : (d + 1) * plane]
    slabs = slab_ref[...]
    high = slabs.astype(BF16)
    rest = slabs - high.astype(F32)
    middle = rest.astype(BF16)
    low = (rest - middle.astype(F32)).astype(BF16)
    lanes = iota((1, row_span * 128), 1)
    slot = lanes % 128 // WT
    wanted = jnp.where(slot < col_span, lanes // 128 * col_span + (col_span - 1) - slot, -1)
    pick = (iota((plane, row_span * 128), 0) == wanted).astype(F32).astype(BF16)
    spread = (dot(low, pick) + dot(middle, pick)) + dot(high, pick)
    for p in range(row_span):
        spread_ref[p] = spread[:, p * 128 : (p + 1) * 128]
    lane_time = iota((WT, 128), 1) % WT
    for h in range(HEADS):
        for p in range(row_span):
            skewed = None
            for a in range(WT):
                rows = spread_ref[p, pl.ds((WT - 1 - a) * HEADS + h, WT, stride=HEADS), :]
                skewed = rows if skewed is None else jnp.where(lane_time == a, rows, skewed)
            skew_ref[h, p] = skewed
    first = iota((WT, 128), 1) < 64
    for h in range(HEADS):
        for d in range(row_span):
            one, two = skew_ref[h, d], skew_ref[h, max(d - 1, 0)]
            for c in range(WW):
                shift = WT * (WW - 1 - c)
                bias_ref[h, d, c] = jnp.where(
                    first,
                    one if shift == 0 else pltpu.roll(one, 128 - shift, 1),
                    pltpu.roll(two, 64 - shift, 1),
                )


def region_classes(shape, row, col, time):
    last_time = lax.axis_index("tm") == TM - 1
    last_row = lax.axis_index("tile") // TCOLS == TROWS - 1
    last_col = lax.axis_index("tile") % TCOLS == TCOLS - 1
    return (
        jnp.where(time >= ST, jnp.where(last_time, 4, 0), 0)
        + jnp.where(row >= WH - SH, jnp.where(last_row, 2, 0), 0)
        + jnp.where(col >= WW - SW, jnp.where(last_col, 1, 0), 0)
    )


def pad_keys(values):
    blocks = values.reshape(WH, WW, WT, CHAN)
    blocks = jnp.concatenate([blocks, jnp.zeros((WH, 1, WT, CHAN), values.dtype)], axis=1)
    blocks = jnp.concatenate([blocks, jnp.zeros((1, 8, WT, CHAN), values.dtype)], axis=0)
    return blocks.reshape(KEYS, CHAN)


def unpad_keys(values):
    return values.reshape(8, 8, WT, CHAN)[:WH, :WW].reshape(TOK, CHAN)


def kernel(
    clip_ref,
    goal_ref,
    from_tile_ref,
    from_window_ref,
    to_tile_ref,
    to_window_ref,
    gain1_ref,
    shift1_ref,
    qkv_weight_ref,
    qkv_bias_ref,
    table_ref,
    proj_weight_ref,
    proj_bias_ref,
    gain2_ref,
    shift2_ref,
    fc1_weight_ref,
    fc1_bias_ref,
    fc2_weight_ref,
    fc2_bias_ref,
    out_ref,
    clip_out,
    clip_in,
    goal_out,
    goal_in,
    back_out,
    back_in,
    slab_ref,
    spread_ref,
    skew_ref,
    bias_ref,
    probs_ref,
    work_ref,
    send_sems,
    recv_sems,
):
    barrier = pltpu.get_barrier_semaphore()
    for cut, _, _, _, _ in AWAY:
        pl.semaphore_signal(barrier, inc=1, device_id=neighbour(1, cut), device_id_type=MESH)

    from_tile = from_tile_ref[...]
    clip_packed = dot(from_tile, clip_ref[...].reshape(TOK, CHAN)).astype(BF16)
    goal_packed = dot(from_tile, goal_ref[...].reshape(TOK, CHAN)).astype(BF16)
    clip_out[...] = clip_packed
    goal_out[...] = goal_packed
    pl.semaphore_wait(barrier, len(AWAY))
    clip_copies = copies(clip_out, clip_in, send_sems.at[0], recv_sems.at[0], -1)
    goal_copies = copies(goal_out, goal_in, send_sems.at[1], recv_sems.at[1], -1)
    for copy in clip_copies:
        copy.start()
    for copy in goal_copies:
        copy.start()
    kept = PLAN[0][2]
    clip_in[0:kept, :] = clip_packed[0:kept]
    goal_in[0:kept, :] = goal_packed[0:kept]

    fill_bias(table_ref[...], slab_ref, spread_ref, skew_ref, bias_ref)

    lane = iota((1, CHAN), 1)
    heads = [(lane // HEAD == h) for h in range(HEADS)]
    heads_low = [mask.astype(F32).astype(BF16) for mask in heads]
    places = [lane - (h + 1) % HEADS * HEAD for h in range(HEADS)]
    token = iota((TOK, 1), 0)
    query_class = region_classes(
        (TOK, 1), token // SLAB, token % SLAB // WT, token % WT
    )
    key = iota((KEYS, 1), 0)
    key_row, key_col = key // 64, key % 64 // WT
    key_class = region_classes((KEYS, 1), key_row, key_col, key % WT)
    key_class = jnp.where((key_row < WH) & (key_col < WW), key_class, 8)

    for copy in clip_copies:
        copy.wait_recv()
    to_window = to_window_ref[...]
    frames = dot(to_window, clip_in[...])
    normal1, inv_std1 = norm_stats(frames)
    normed1 = (normal1 * gain1_ref[...] + shift1_ref[...]).astype(BF16)
    projected = dot(normed1, qkv_weight_ref[...]) + qkv_bias_ref[...]
    queries = projected[:, :CHAN] * SCALE
    keys = pad_keys(projected[:, CHAN : 2 * CHAN])
    values = pad_keys(projected[:, 2 * CHAN :]).astype(BF16)
    queries_low = queries.astype(BF16)
    keys_low = keys.astype(BF16)

    mixed = None
    for h in range(HEADS):
        query_extra = ((query_class == places[h]) & (places[h] >= 0)).astype(F32)
        key_extra = jnp.where(
            (key_class != places[h]) & (places[h] >= 0) & (places[h] < 8), MASKED, 0.0
        )
        head_queries = jnp.where(heads[h], queries, query_extra).astype(BF16)
        head_keys = jnp.where(heads[h], keys, key_extra).astype(BF16)
        work_ref[h] = dot(head_queries, head_keys, NT)
        for b in range(WH):
            span = pl.ds(b * SLAB, SLAB)
            scores = work_ref[h, span, :]
            bias = jnp.concatenate(
                [bias_ref[h, b - 2 * m + 6].reshape(SLAB, 128) for m in range(4)], axis=1
            )
            scores = scores + bias
            exponent = jnp.exp(scores - jnp.max(scores, -1, keepdims=True))
            probs_ref[h, span, :] = exponent * (1.0 / jnp.sum(exponent, -1, keepdims=True))
        part = dot(probs_ref[h].astype(BF16), values * heads_low[h])
        mixed = part if mixed is None else mixed + part
    mixed = mixed.astype(BF16)
    branch = (dot(mixed, proj_weight_ref[...]) + proj_bias_ref[...]).astype(BF16)
    ys = frames + branch.astype(F32)

    normal2, inv_std2 = norm_stats(ys)
    normed2 = (normal2 * gain2_ref[...] + shift2_ref[...]).astype(BF16)
    work_ref[0] = dot(normed2, fc1_weight_ref[...]) + fc1_bias_ref[...]
    for b in range(WH):
        span = pl.ds(b * SLAB, SLAB)
        pre_act = work_ref[0, span, :]
        half = 0.5 * (1.0 + lax.erf(pre_act * ROOT_HALF))
        work_ref[1, span, :] = pre_act * half
        work_ref[2, span, :] = half + pre_act * INV_ROOT_TAU * jnp.exp(-0.5 * pre_act * pre_act)
    outputs = ys + dot(work_ref[1].astype(BF16), fc2_weight_ref[...]) + fc2_bias_ref[...]
    for copy in goal_copies:
        copy.wait_recv()
    goal = dot(to_window, goal_in[...])
    grad_out = outputs - goal
    grad_pre = (dot(grad_out.astype(BF16), fc2_weight_ref[...], NT) * work_ref[2]).astype(BF16)
    grad_norm2 = dot(grad_pre, fc1_weight_ref[...], NT)
    grad_ys = grad_out + norm_backward(grad_norm2, normal2, inv_std2, gain2_ref[...])

    grad_mixed = dot(grad_ys.astype(BF16), proj_weight_ref[...], NT)
    grad_mixed_low = grad_mixed.astype(BF16)
    queries_across = queries.T.astype(BF16)
    grad_mixed_across = grad_mixed.T.astype(BF16)
    grad_queries = None
    grad_keys = []
    grad_values = []
    for h in range(HEADS):
        rows = slice(h * HEAD, (h + 1) * HEAD)
        work_ref[h] = dot(grad_mixed_low * heads_low[h], values, NT)
        for b in range(WH):
            span = pl.ds(b * SLAB, SLAB)
            probs = probs_ref[h, span, :]
            grad_probs = work_ref[h, span, :]
            delta = jnp.sum(probs * grad_probs, -1, keepdims=True)
            work_ref[h, span, :] = probs * (grad_probs - delta)
        grad_scores = work_ref[h].astype(BF16)
        part = dot(grad_scores, keys_low * heads_low[h])
        grad_queries = part if grad_queries is None else grad_queries + part
        grad_keys.append(dot(queries_across[rows], grad_scores))
        grad_values.append(dot(grad_mixed_across[rows], probs_ref[h].astype(BF16)))
    grad_queries = (grad_queries * SCALE).astype(BF16)
    grad_keys = unpad_keys(jnp.concatenate(grad_keys, axis=0).T).astype(BF16)
    grad_values = unpad_keys(jnp.concatenate(grad_values, axis=0).T).astype(BF16)
    grad_qkv = jnp.concatenate([grad_queries, grad_keys, grad_values], axis=1)
    grad_normed = dot(grad_qkv, qkv_weight_ref[...], NT).astype(BF16).astype(F32)
    result = grad_ys + norm_backward(grad_normed, normal1, inv_std1, gain1_ref[...])

    back_packed = dot(from_window_ref[...], result.astype(BF16)).astype(BF16)
    back_out[...] = back_packed
    back_copies = copies(back_out, back_in, send_sems.at[2], recv_sems.at[2], 1)
    for copy in back_copies:
        copy.start()
    back_in[0:kept, :] = back_packed[0:kept]
    for copy in back_copies:
        copy.wait_recv()
    out_ref[...] = dot(to_tile_ref[...], back_in[...]).astype(BF16).reshape(WH * WW, WT, CHAN)
    for copy in clip_copies + goal_copies + back_copies:
        copy.wait_send()


def shards(
    clip_tokens,
    target,
    norm1_gain,
    norm1_bias,
    qkv_weight,
    qkv_bias,
    bias_table,
    proj_weight,
    proj_bias,
    norm2_gain,
    norm2_bias,
    fc1_weight,
    fc1_bias,
    fc2_weight,
    fc2_bias,
):
    def by_place(tokens):
        return jnp.transpose(tokens, (1, 2, 3, 0, 4)).reshape(WH * WW, WT, CHAN)

    from_tile, from_window = selectors()
    operands = [
        by_place(clip_tokens),
        by_place(target),
        jnp.asarray(from_tile, BF16),
        jnp.asarray(from_window, BF16),
        jnp.asarray(from_tile.T, BF16),
        jnp.asarray(from_window.T, BF16),
        norm1_gain.reshape(1, -1),
        norm1_bias.reshape(1, -1),
        qkv_weight,
        qkv_bias.reshape(1, -1),
        bias_table.T,
        proj_weight,
        proj_bias.reshape(1, -1),
        norm2_gain.reshape(1, -1),
        norm2_bias.reshape(1, -1),
        fc1_weight,
        fc1_bias.reshape(1, -1),
        fc2_weight,
        fc2_bias.reshape(1, -1),
    ]
    vmem = pl.BlockSpec(memory_space=pltpu.VMEM)
    plane = (2 * WH - 1) * (2 * WW - 1)
    out = pl.pallas_call(
        kernel,
        out_shape=jax.ShapeDtypeStruct((WH * WW, WT, CHAN), BF16),
        in_specs=[vmem] * len(operands),
        out_specs=vmem,
        scratch_shapes=[pltpu.VMEM((PACKED, CHAN), BF16)] * 6
        + [
            pltpu.VMEM((HEADS * (2 * WT - 1), plane), F32),
            pltpu.VMEM((2 * WH - 1, HEADS * (2 * WT - 1), 128), F32),
            pltpu.VMEM((HEADS, 2 * WH - 1, WT, 128), F32),
            pltpu.VMEM((HEADS, 2 * WH - 1, WW, WT, 128), F32),
            pltpu.VMEM((HEADS, TOK, KEYS), F32),
            pltpu.VMEM((HEADS, TOK, KEYS), F32),
            pltpu.SemaphoreType.DMA((3, len(AWAY))),
            pltpu.SemaphoreType.DMA((3, len(AWAY))),
        ],
        compiler_params=pltpu.CompilerParams(
            collective_id=0, has_side_effects=True, vmem_limit_bytes=48 * 1024 * 1024
        ),
        name="window_block",
    )(*operands)
    return jnp.transpose(out.reshape(1, WH, WW, WT, CHAN), (3, 0, 1, 2, 4))


def solution(mesh):
    return jax.shard_map(
        shards,
        mesh=mesh,
        in_specs=(P("tm", "tile", None, None, None),) * 2 + (P(),) * 13,
        out_specs=P("tm", "tile", None, None, None),
        check_vma=False,
    )
```

profile of v0, /device:TPU:32, one launch (start us, length us, event | category | flops | bytes accessed | tf_op | source)
XLA Modules:
  0.0 44.1 jit_solution(13474629260785237735)
XLA Ops:
  0.0 0.0 copy-start.18
  0.0 0.0 copy-start.15
  0.0 0.0 copy-start.16
  0.0 0.0 copy-start.17
  0.0 0.7 %copy-done.18 = f32[384]{0:T(512)S(1)} copy-done((f32[384]{0:T(512)S(1)}, f32[384]{0:T(512)}, u32[]{:S(2)}) %copy-start.18) | copy-done | bytes 1560
  0.7 0.0 copy-start.11
  0.7 0.0 copy-start.12
  0.7 0.0 copy-start.13
  0.7 0.0 copy-start.14
  0.7 0.0 copy-done.15
  0.7 0.0 copy-done.16
  0.7 0.0 copy-done.17
  0.7 0.6 %copy-done.11 = f32[512]{0:T(512)S(1)} copy-done((f32[512]{0:T(512)S(1)}, f32[512]{0:T(512)}, u32[]{:S(2)}) %copy-start.11) | copy-done | bytes 2072
  1.4 0.0 copy-done.12
  1.4 0.0 copy-done.13
  1.4 0.0 copy-done.14
  1.4 0.0 copy-start
  1.4 1.0 %copy-done = bf16[416,392]{1,0:T(8,128)(2,1)S(1)} copy-done((bf16[416,392]{1,0:T(8,128)(2,1)S(1)}, bf16[416,392]{1,0:T(8,128)(2,1)}, u32[]{:S(2)}) %copy-start) | copy-done | bytes 326168
  2.4 0.0 copy-start.1
  2.4 1.0 %copy-done.1 = bf16[416,392]{1,0:T(8,128)(2,1)S(1)} copy-done((bf16[416,392]{1,0:T(8,128)(2,1)S(1)}, bf16[416,392]{1,0:T(8,128)(2,1)}, u32[]{:S(2)}) %copy-start.1) | copy-done | bytes 326168
  3.4 0.0 copy-start.2
  3.4 1.0 %copy-done.2 = bf16[392,416]{1,0:T(8,128)(2,1)S(1)} copy-done((bf16[392,416]{1,0:T(8,128)(2,1)S(1)}, bf16[392,416]{1,0:T(8,128)(2,1)}, u32[]{:S(2)}) %copy-start.2) | copy-done | bytes 326168
  4.4 0.0 copy-start.3
  4.4 1.0 %copy-done.3 = bf16[392,416]{1,0:T(8,128)(2,1)S(1)} copy-done((bf16[392,416]{1,0:T(8,128)(2,1)S(1)}, bf16[392,416]{1,0:T(8,128)(2,1)}, u32[]{:S(2)}) %copy-start.3) | copy-done | bytes 326168
  5.4 0.0 copy-start.4
  5.4 0.9 %copy-done.4 = bf16[128,512]{1,0:T(8,128)(2,1)S(1)} copy-done((bf16[128,512]{1,0:T(8,128)(2,1)S(1)}, bf16[128,512]{1,0:T(8,128)(2,1)}, u32[]{:S(2)}) %copy-start.4) | copy-done | bytes 131096
  6.3 0.0 copy-start.5
  6.3 0.9 %copy-done.5 = bf16[512,128]{1,0:T(8,128)(2,1)S(1)} copy-done((bf16[512,128]{1,0:T(8,128)(2,1)S(1)}, bf16[512,128]{1,0:T(8,128)(2,1)}, u32[]{:S(2)}) %copy-start.5) | copy-done | bytes 131096
  7.2 0.0 copy-start.6
  7.2 0.9 %copy-done.6 = bf16[8,1,7,7,128]{4,0,3,2,1:T(8,128)(2,1)S(1)} copy-done((bf16[8,1,7,7,128]{4,0,3,2,1:T(8,128)(2,1)S(1)}, bf16[8,1,7,7,128]{4,0,3,2,1:T(8,128)(2,1)}, u32[]{:S(2)}) %copy-start.6) | copy-done | bytes 100376
  8.1 0.0 copy-start.7
  8.1 0.9 %copy-done.7 = bf16[8,1,7,7,128]{4,0,3,2,1:T(8,128)(2,1)S(1)} copy-done((bf16[8,1,7,7,128]{4,0,3,2,1:T(8,128)(2,1)S(1)}, bf16[8,1,7,7,128]{4,0,3,2,1:T(8,128)(2,1)}, u32[]{:S(2)}) %copy-start.7) | copy-done | bytes 100376
  9.0 0.0 copy-start.8
  9.0 0.9 %copy-done.8 = bf16[128,384]{1,0:T(8,128)(2,1)S(1)} copy-done((bf16[128,384]{1,0:T(8,128)(2,1)S(1)}, bf16[128,384]{1,0:T(8,128)(2,1)}, u32[]{:S(2)}) %copy-start.8) | copy-done | bytes 98328
  9.9 0.0 copy-start.9
  9.9 0.8 %copy-done.9 = f32[2535,4]{0,1:T(4,128)S(1)} copy-done((f32[2535,4]{0,1:T(4,128)S(1)}, f32[2535,4]{0,1:T(4,128)}, u32[]{:S(2)}) %copy-start.9) | copy-done | bytes 40584
  10.7 0.0 copy-start.10
  10.7 0.8 %copy-done.10 = bf16[128,128]{1,0:T(8,128)(2,1)S(1)} copy-done((bf16[128,128]{1,0:T(8,128)(2,1)S(1)}, bf16[128,128]{1,0:T(8,128)(2,1)}, u32[]{:S(2)}) %copy-start.10) | copy-done | bytes 32792
  11.4 32.0 %window_block.1 = bf16[49,8,128]{2,1,0:T(8,128)(2,1)S(1)} custom-call(bf16[49,8,128]{2,1,0:T(8,128)(2,1)S(1)} %bitcast.18, bf16[49,8,128]{2,1,0:T(8,128)(2,1)S(1)} %bitcast.19, bf16[416,392]{1,0:T(8,128)(2,1)S(1)} %copy-done.1, bf16[416,392]{1,0:T(8,128)(2,1)S(1)} %copy-done, bf16[392,416]{1,0:T(8,128)(2,1)S(1)} %copy-done.3, ...), custom_call_target="tpu_custom_call" | custom-call | tf_op jit(solution)/shard_map/window_block/pallas_call | solution.py:394
  43.5 0.6 %copy.21 = bf16[8,1,7,7,128]{4,0,3,2,1:T(8,128)(2,1)} copy(bf16[8,1,7,7,128]{4,0,3,2,1:T(8,128)(2,1)S(1)} %bitcast.17) | data formatting | bytes 200704
  (1 shorter events, 0.0 us)
Async XLA Ops:
  0.0 0.7 %copy-start.18 = (f32[384]{0:T(512)S(1)}, f32[384]{0:T(512)}, u32[]{:S(2)}) copy-start(f32[384]{0:T(512)} %param.24) | copy-start | bytes 4612
  0.0 0.7 %copy-start.15 = (f32[128]{0:T(128)S(1)}, f32[128]{0:T(128)}, u32[]{:S(2)}) copy-start(f32[128]{0:T(128)} %param.28) | copy-start | bytes 1540
  0.0 0.7 %copy-start.16 = (f32[128]{0:T(128)S(1)}, f32[128]{0:T(128)}, u32[]{:S(2)}) copy-start(f32[128]{0:T(128)} %param.29) | copy-start | bytes 1540
  0.0 0.7 %copy-start.17 = (f32[128]{0:T(128)S(1)}, f32[128]{0:T(128)}, u32[]{:S(2)}) copy-start(f32[128]{0:T(128)} %param.33) | copy-start | bytes 1540
  0.7 0.7 %copy-start.11 = (f32[512]{0:T(512)S(1)}, f32[512]{0:T(512)}, u32[]{:S(2)}) copy-start(f32[512]{0:T(512)} %param.31) | copy-start | bytes 6148
  0.7 0.7 %copy-start.12 = (f32[128]{0:T(128)S(1)}, f32[128]{0:T(128)}, u32[]{:S(2)}) copy-start(f32[128]{0:T(128)} %param.21) | copy-start | bytes 1540
  0.7 0.7 %copy-start.13 = (f32[128]{0:T(128)S(1)}, f32[128]{0:T(128)}, u32[]{:S(2)}) copy-start(f32[128]{0:T(128)} %param.22) | copy-start | bytes 1540
  0.7 0.7 %copy-start.14 = (f32[128]{0:T(128)S(1)}, f32[128]{0:T(128)}, u32[]{:S(2)}) copy-start(f32[128]{0:T(128)} %param.27) | copy-start | bytes 1540
  1.4 1.0 %copy-start = (bf16[416,392]{1,0:T(8,128)(2,1)S(1)}, bf16[416,392]{1,0:T(8,128)(2,1)}, u32[]{:S(2)}) copy-start(bf16[416,392]{1,0:T(8,128)(2,1)} %constant.9.clone.from_window_ref) | copy-start | bytes 978436
  2.4 1.0 %copy-start.1 = (bf16[416,392]{1,0:T(8,128)(2,1)S(1)}, bf16[416,392]{1,0:T(8,128)(2,1)}, u32[]{:S(2)}) copy-start(bf16[416,392]{1,0:T(8,128)(2,1)} %constant.8.clone.from_tile_ref) | copy-start | bytes 978436
  3.4 1.0 %copy-start.2 = (bf16[392,416]{1,0:T(8,128)(2,1)S(1)}, bf16[392,416]{1,0:T(8,128)(2,1)}, u32[]{:S(2)}) copy-start(bf16[392,416]{1,0:T(8,128)(2,1)} %constant.11.clone.to_window_ref) | copy-start | bytes 978436
  4.4 1.0 %copy-start.3 = (bf16[392,416]{1,0:T(8,128)(2,1)S(1)}, bf16[392,416]{1,0:T(8,128)(2,1)}, u32[]{:S(2)}) copy-start(bf16[392,416]{1,0:T(8,128)(2,1)} %constant.10.clone.to_tile_ref) | copy-start | bytes 978436
  5.4 0.9 %copy-start.4 = (bf16[128,512]{1,0:T(8,128)(2,1)S(1)}, bf16[128,512]{1,0:T(8,128)(2,1)}, u32[]{:S(2)}) copy-start(bf16[128,512]{1,0:T(8,128)(2,1)} %fc1_weight_ref.1) | copy-start | bytes 393220
  6.3 0.9 %copy-start.5 = (bf16[512,128]{1,0:T(8,128)(2,1)S(1)}, bf16[512,128]{1,0:T(8,128)(2,1)}, u32[]{:S(2)}) copy-start(bf16[512,128]{1,0:T(8,128)(2,1)} %fc2_weight_ref.1) | copy-start | bytes 393220
  7.2 0.9 %copy-start.6 = (bf16[8,1,7,7,128]{4,0,3,2,1:T(8,128)(2,1)S(1)}, bf16[8,1,7,7,128]{4,0,3,2,1:T(8,128)(2,1)}, u32[]{:S(2)}) copy-start(bf16[8,1,7,7,128]{4,0,3,2,1:T(8,128)(2,1)} %param.19) | copy-start | bytes 301060
  8.1 0.9 %copy-start.7 = (bf16[8,1,7,7,128]{4,0,3,2,1:T(8,128)(2,1)S(1)}, bf16[8,1,7,7,128]{4,0,3,2,1:T(8,128)(2,1)}, u32[]{:S(2)}) copy-start(bf16[8,1,7,7,128]{4,0,3,2,1:T(8,128)(2,1)} %param.20) | copy-start | bytes 301060
  9.0 0.9 %copy-start.8 = (bf16[128,384]{1,0:T(8,128)(2,1)S(1)}, bf16[128,384]{1,0:T(8,128)(2,1)}, u32[]{:S(2)}) copy-start(bf16[128,384]{1,0:T(8,128)(2,1)} %qkv_weight_ref.1) | copy-start | bytes 294916
  9.9 0.8 %copy-start.9 = (f32[2535,4]{0,1:T(4,128)S(1)}, f32[2535,4]{0,1:T(4,128)}, u32[]{:S(2)}) copy-start(f32[2535,4]{0,1:T(4,128)} %param.25) | copy-start | bytes 121684
  10.7 0.8 %copy-start.10 = (bf16[128,128]{1,0:T(8,128)(2,1)S(1)}, bf16[128,128]{1,0:T(8,128)(2,1)}, u32[]{:S(2)}) copy-start(bf16[128,128]{1,0:T(8,128)(2,1)} %proj_weight_ref.1) | copy-start | bytes 98308
where the time goes:
time: 44.8 us; the launch traced here: 44.1 us
  Pallas kernels  32 us (71%)
  local copies, waits for them, and re-layouts  12 us (27%)
    pallas_call x1, Pallas kernels, shards(): pl.pallas_call(kernel, out_shape=jax.ShapeDtypeStruct((WH * WW, WT, CHAN)...  32 us
    unnamed x39, local copies, waits for them, and re-layouts  12 us

commit v1 on v0

--- a/solution.py
+++ b/solution.py
@@ -158,7 +158,7 @@
                 )
 
 
-def region_classes(shape, row, col, time):
+def region_classes(row, col, time):
     last_time = lax.axis_index("tm") == TM - 1
     last_row = lax.axis_index("tile") // TCOLS == TROWS - 1
     last_col = lax.axis_index("tile") % TCOLS == TCOLS - 1
@@ -180,88 +180,109 @@
     return values.reshape(8, 8, WT, CHAN)[:WH, :WW].reshape(TOK, CHAN)
 
 
-def kernel(
-    clip_ref,
-    goal_ref,
-    from_tile_ref,
-    from_window_ref,
-    to_tile_ref,
-    to_window_ref,
-    gain1_ref,
-    shift1_ref,
-    qkv_weight_ref,
-    qkv_bias_ref,
-    table_ref,
-    proj_weight_ref,
-    proj_bias_ref,
-    gain2_ref,
-    shift2_ref,
-    fc1_weight_ref,
-    fc1_bias_ref,
-    fc2_weight_ref,
-    fc2_bias_ref,
-    out_ref,
-    clip_out,
-    clip_in,
-    goal_out,
-    goal_in,
-    back_out,
-    back_in,
-    slab_ref,
-    spread_ref,
-    skew_ref,
-    bias_ref,
-    probs_ref,
-    work_ref,
-    send_sems,
-    recv_sems,
-):
+OPERANDS = (
+    "clip",
+    "from_tile",
+    "table",
+    "to_window",
+    "gain1",
+    "shift1",
+    "qkv_weight",
+    "qkv_bias",
+    "goal",
+    "proj_weight",
+    "proj_bias",
+    "gain2",
+    "shift2",
+    "fc1_weight",
+    "fc1_bias",
+    "fc2_weight",
+    "fc2_bias",
+    "from_window",
+    "to_tile",
+)
+
+
+def kernel(*refs):
+    count = len(OPERANDS)
+    sources, out_ref, held = refs[:count], refs[count], refs[count + 1 : 2 * count + 1]
+    (
+        load_sems,
+        clip_out,
+        clip_in,
+        goal_out,
+        goal_in,
+        back_out,
+        back_in,
+        slab_ref,
+        spread_ref,
+        skew_ref,
+        bias_ref,
+        scores_ref,
+        probs_ref,
+        grad_ref,
+        send_sems,
+        recv_sems,
+    ) = refs[2 * count + 1 :]
+
+    loads = {}
+    for i, name in enumerate(OPERANDS):
+        loads[name] = (pltpu.make_async_copy(sources[i], held[i], load_sems.at[i]), held[i])
+        loads[name][0].start()
     barrier = pltpu.get_barrier_semaphore()
     for cut, _, _, _, _ in AWAY:
         pl.semaphore_signal(barrier, inc=1, device_id=neighbour(1, cut), device_id_type=MESH)
 
-    from_tile = from_tile_ref[...]
-    clip_packed = dot(from_tile, clip_ref[...].reshape(TOK, CHAN)).astype(BF16)
-    goal_packed = dot(from_tile, goal_ref[...].reshape(TOK, CHAN)).astype(BF16)
+    def operand(name):
+        copy, ref = loads[name]
+        copy.wait()
+        return ref[...]
+
+    clip = operand("clip").reshape(TOK, CHAN)
+    from_tile = operand("from_tile")[:PACKED]
+    clip_packed = dot(from_tile, clip).astype(BF16)
     clip_out[...] = clip_packed
-    goal_out[...] = goal_packed
     pl.semaphore_wait(barrier, len(AWAY))
     clip_copies = copies(clip_out, clip_in, send_sems.at[0], recv_sems.at[0], -1)
-    goal_copies = copies(goal_out, goal_in, send_sems.at[1], recv_sems.at[1], -1)
     for copy in clip_copies:
-        copy.start()
-    for copy in goal_copies:
         copy.start()
     kept = PLAN[0][2]
     clip_in[0:kept, :] = clip_packed[0:kept]
+
+    goal_packed = dot(from_tile, operand("goal").reshape(TOK, CHAN)).astype(BF16)
+    goal_out[...] = goal_packed
+    goal_copies = copies(goal_out, goal_in, send_sems.at[1], recv_sems.at[1], -1)
+    for copy in goal_copies:
+        copy.start()
     goal_in[0:kept, :] = goal_packed[0:kept]
 
-    fill_bias(table_ref[...], slab_ref, spread_ref, skew_ref, bias_ref)
+    fill_bias(operand("table"), slab_ref, spread_ref, skew_ref, bias_ref)
 
     lane = iota((1, CHAN), 1)
     heads = [(lane // HEAD == h) for h in range(HEADS)]
     heads_low = [mask.astype(F32).astype(BF16) for mask in heads]
     places = [lane - (h + 1) % HEADS * HEAD for h in range(HEADS)]
     token = iota((TOK, 1), 0)
-    query_class = region_classes(
-        (TOK, 1), token // SLAB, token % SLAB // WT, token % WT
-    )
+    query_class = region_classes(token // SLAB, token % SLAB // WT, token % WT)
     key = iota((KEYS, 1), 0)
     key_row, key_col = key // 64, key % 64 // WT
-    key_class = region_classes((KEYS, 1), key_row, key_col, key % WT)
+    key_class = region_classes(key_row, key_col, key % WT)
     key_class = jnp.where((key_row < WH) & (key_col < WW), key_class, 8)
 
+    to_window = operand("to_window")
+    gain1 = operand("gain1")
+    shift1 = operand("shift1")
+    qkv_weight = operand("qkv_weight")
+    qkv_bias = operand("qkv_bias")
     for copy in clip_copies:
         copy.wait_recv()
-    to_window = to_window_ref[...]
     frames = dot(to_window, clip_in[...])
     normal1, inv_std1 = norm_stats(frames)
-    normed1 = (normal1 * gain1_ref[...] + shift1_ref[...]).astype(BF16)
-    projected = dot(normed1, qkv_weight_ref[...]) + qkv_bias_ref[...]
-    queries = projected[:, :CHAN] * SCALE
-    keys = pad_keys(projected[:, CHAN : 2 * CHAN])
-    values = pad_keys(projected[:, 2 * CHAN :]).astype(BF16)
-    queries_low = queries.astype(BF16)
+    normed1 = (normal1 * gain1 + shift1).astype(BF16)
+    projected = dot(normed1, qkv_weight)
+    queries = (projected[:, :CHAN] + qkv_bias[0:1]) * SCALE
+    keys = pad_keys(projected[:, CHAN : 2 * CHAN] + qkv_bias[1:2])
+    values = pad_keys(projected[:, 2 * CHAN :] + qkv_bias[2:3]).astype(BF16)
     keys_low = keys.astype(BF16)
 
     mixed = None
@@ -272,42 +293,55 @@
         )
         head_queries = jnp.where(heads[h], queries, query_extra).astype(BF16)
         head_keys = jnp.where(heads[h], keys, key_extra).astype(BF16)
-        work_ref[h] = dot(head_queries, head_keys, NT)
-        for b in range(WH):
-            span = pl.ds(b * SLAB, SLAB)
-            scores = work_ref[h, span, :]
+        scores_ref[h] = dot(head_queries, head_keys, NT)
+        for first in range(0, WH, 2):
+            slabs = range(first, min(first + 2, WH))
+            span = pl.ds(first * SLAB, len(slabs) * SLAB)
             bias = jnp.concatenate(
-                [bias_ref[h, b - 2 * m + 6].reshape(SLAB, 128) for m in range(4)], axis=1
+                [
+                    jnp.concatenate(
+                        [bias_ref[h, b - 2 * m + 6].reshape(SLAB, 128) for m in range(4)], axis=1
+                    )
+                    for b in slabs
+                ],
+                axis=0,
             )
-            scores = scores + bias
+            scores = scores_ref[h, span, :] + bias
             exponent = jnp.exp(scores - jnp.max(scores, -1, keepdims=True))
-            probs_ref[h, span, :] = exponent * (1.0 / jnp.sum(exponent, -1, keepdims=True))
-        part = dot(probs_ref[h].astype(BF16), values * heads_low[h])
+            probs_ref[h, span, :] = exponent.astype(BF16)
+        ones = jnp.broadcast_to(heads_low[h], (KEYS, CHAN))
+        part = dot(probs_ref[h], jnp.concatenate([values * heads_low[h], ones], axis=1))
         mixed = part if mixed is None else mixed + part
-    mixed = mixed.astype(BF16)
-    branch = (dot(mixed, proj_weight_ref[...]) + proj_bias_ref[...]).astype(BF16)
+    inv_total = 1.0 / mixed[:, CHAN:]
+    mixed = mixed[:, :CHAN] * inv_total
+    proj_weight = operand("proj_weight")
+    branch = (dot(mixed.astype(BF16), proj_weight) + operand("proj_bias")).astype(BF16)
     ys = frames + branch.astype(F32)
 
+    gain2 = operand("gain2")
+    fc1_weight = operand("fc1_weight")
+    fc2_weight = operand("fc2_weight")
     normal2, inv_std2 = norm_stats(ys)
-    normed2 = (normal2 * gain2_ref[...] + shift2_ref[...]).astype(BF16)
-    work_ref[0] = dot(normed2, fc1_weight_ref[...]) + fc1_bias_ref[...]
+    normed2 = (normal2 * gain2 + operand("shift2")).astype(BF16)
+    scores_ref[0] = dot(normed2, fc1_weight) + operand("fc1_bias")
     for b in range(WH):
         span = pl.ds(b * SLAB, SLAB)
-        pre_act = work_ref[0, span, :]
+        pre_act = scores_ref[0, span, :]
         half = 0.5 * (1.0 + lax.erf(pre_act * ROOT_HALF))
-        work_ref[1, span, :] = pre_act * half
-        work_ref[2, span, :] = half + pre_act * INV_ROOT_TAU * jnp.exp(-0.5 * pre_act * pre_act)
-    outputs = ys + dot(work_ref[1].astype(BF16), fc2_weight_ref[...]) + fc2_bias_ref[...]
+        scores_ref[1, span, :] = pre_act * half
+        scores_ref[2, span, :] = half + pre_act * INV_ROOT_TAU * jnp.exp(-0.5 * pre_act * pre_act)
+    outputs = ys + dot(scores_ref[1].astype(BF16), fc2_weight) + operand("fc2_bias")
     for copy in goal_copies:
         copy.wait_recv()
     goal = dot(to_window, goal_in[...])
     grad_out = outputs - goal
-    grad_pre = (dot(grad_out.astype(BF16), fc2_weight_ref[...], NT) * work_ref[2]).astype(BF16)
-    grad_norm2 = dot(grad_pre, fc1_weight_ref[...], NT)
-    grad_ys = grad_out + norm_backward(grad_norm2, normal2, inv_std2, gain2_ref[...])
-
-    grad_mixed = dot(grad_ys.astype(BF16), proj_weight_ref[...], NT)
+    grad_pre = (dot(grad_out.astype(BF16), fc2_weight, NT) * scores_ref[2]).astype(BF16)
+    grad_norm2 = dot(grad_pre, fc1_weight, NT)
+    grad_ys = grad_out + norm_backward(grad_norm2, normal2, inv_std2, gain2)
+
+    grad_mixed = dot(grad_ys.astype(BF16), proj_weight, NT) * inv_total
     grad_mixed_low = grad_mixed.astype(BF16)
+    toward = grad_mixed_low.astype(F32) * mixed
     queries_across = queries.T.astype(BF16)
     grad_mixed_across = grad_mixed.T.astype(BF16)
     grad_queries = None
@@ -315,34 +349,37 @@
     grad_values = []
     for h in range(HEADS):
         rows = slice(h * HEAD, (h + 1) * HEAD)
-        work_ref[h] = dot(grad_mixed_low * heads_low[h], values, NT)
-        for b in range(WH):
-            span = pl.ds(b * SLAB, SLAB)
-            probs = probs_ref[h, span, :]
-            grad_probs = work_ref[h, span, :]
-            delta = jnp.sum(probs * grad_probs, -1, keepdims=True)
-            work_ref[h, span, :] = probs * (grad_probs - delta)
-        grad_scores = work_ref[h].astype(BF16)
+        delta = jnp.sum(jnp.where(heads[h], toward, 0.0), -1, keepdims=True)
+        scores_ref[h] = dot(grad_mixed_low * heads_low[h], values, NT)
+        for first in range(0, WH, 2):
+            rows_here = slice(first * SLAB, min(first + 2, WH) * SLAB)
+            span = pl.ds(first * SLAB, rows_here.stop - rows_here.start)
+            probs = probs_ref[h, span, :].astype(F32)
+            grad_ref[h, span, :] = (
+                probs * (scores_ref[h, span, :] - delta[rows_here])
+            ).astype(BF16)
+        grad_scores = grad_ref[h]
         part = dot(grad_scores, keys_low * heads_low[h])
         grad_queries = part if grad_queries is None else grad_queries + part
         grad_keys.append(dot(queries_across[rows], grad_scores))
-        grad_values.append(dot(grad_mixed_across[rows], probs_ref[h].astype(BF16)))
+        grad_values.append(dot(grad_mixed_across[rows], probs_ref[h]))
     grad_queries = (grad_queries * SCALE).astype(BF16)
     grad_keys = unpad_keys(jnp.concatenate(grad_keys, axis=0).T).astype(BF16)
     grad_values = unpad_keys(jnp.concatenate(grad_values, axis=0).T).astype(BF16)
     grad_qkv = jnp.concatenate([grad_queries, grad_keys, grad_values], axis=1)
-    grad_normed = dot(grad_qkv, qkv_weight_ref[...], NT).astype(BF16).astype(F32)
-    result = grad_ys + norm_backward(grad_normed, normal1, inv_std1, gain1_ref[...])
-
-    back_packed = dot(from_window_ref[...], result.astype(BF16)).astype(BF16)
+    grad_normed = dot(grad_qkv, qkv_weight, NT).astype(BF16).astype(F32)
+    result = grad_ys + norm_backward(grad_normed, normal1, inv_std1, gain1)
+
+    back_packed = dot(operand("from_window")[:PACKED], result.astype(BF16)).astype(BF16)
     back_out[...] = back_packed
     back_copies = copies(back_out, back_in, send_sems.at[2], recv_sems.at[2], 1)
     for copy in back_copies:
         copy.start()
     back_in[0:kept, :] = back_packed[0:kept]
+    to_tile = operand("to_tile")
     for copy in back_copies:
         copy.wait_recv()
-    out_ref[...] = dot(to_tile_ref[...], back_in[...]).astype(BF16).reshape(WH * WW, WT, CHAN)
+    out_ref[...] = dot(to_tile, back_in[...]).astype(BF16).reshape(WH * WW, WT, CHAN)
     for copy in clip_copies + goal_copies + back_copies:
         copy.wait_send()
 
@@ -368,47 +405,50 @@
         return jnp.transpose(tokens, (1, 2, 3, 0, 4)).reshape(WH * WW, WT, CHAN)
 
     from_tile, from_window = selectors()
-    operands = [
-        by_place(clip_tokens),
-        by_place(target),
-        jnp.asarray(from_tile, BF16),
-        jnp.asarray(from_window, BF16),
-        jnp.asarray(from_tile.T, BF16),
-        jnp.asarray(from_window.T, BF16),
-        norm1_gain.reshape(1, -1),
-        norm1_bias.reshape(1, -1),
-        qkv_weight,
-        qkv_bias.reshape(1, -1),
-        bias_table.T,
-        proj_weight,
-        proj_bias.reshape(1, -1),
-        norm2_gain.reshape(1, -1),
-        norm2_bias.reshape(1, -1),
-        fc1_weight,
-        fc1_bias.reshape(1, -1),
-        fc2_weight,
-        fc2_bias.reshape(1, -1),
-    ]
-    vmem = pl.BlockSpec(memory_space=pltpu.VMEM)
+    named = {
+        "clip": by_place(clip_tokens),
+        "from_tile": jnp.asarray(np.pad(from_tile, ((0, 8), (0, 0))), BF16),
+        "table": bias_table.T,
+        "to_window": jnp.asarray(from_window.T, BF16),
+        "gain1": norm1_gain.reshape(1, -1),
+        "shift1": norm1_bias.reshape(1, -1),
+        "qkv_weight": qkv_weight,
+        "qkv_bias": qkv_bias.reshape(3, -1),
+        "goal": by_place(target),
+        "proj_weight": proj_weight,
+        "proj_bias": proj_bias.reshape(1, -1),
+        "gain2": norm2_gain.reshape(1, -1),
+        "shift2": norm2_bias.reshape(1, -1),
+        "fc1_weight": fc1_weight,
+        "fc1_bias": fc1_bias.reshape(1, -1),
+        "fc2_weight": fc2_weight,
+        "fc2_bias": fc2_bias.reshape(1, -1),
+        "from_window": jnp.asarray(np.pad(from_window, ((0, 8), (0, 0))), BF16),
+        "to_tile": jnp.asarray(from_tile.T, BF16),
+    }
+    operands = [named[name] for name in OPERANDS]
     plane = (2 * WH - 1) * (2 * WW - 1)
     out = pl.pallas_call(
         kernel,
         out_shape=jax.ShapeDtypeStruct((WH * WW, WT, CHAN), BF16),
-        in_specs=[vmem] * len(operands),
-        out_specs=vmem,
-        scratch_shapes=[pltpu.VMEM((PACKED, CHAN), BF16)] * 6
+        in_specs=[pl.BlockSpec(memory_space=pltpu.HBM)] * len(operands),
+        out_specs=pl.BlockSpec(memory_space=pltpu.VMEM),
+        scratch_shapes=[pltpu.VMEM(x.shape, x.dtype) for x in operands]
+        + [pltpu.SemaphoreType.DMA((len(operands),))]
+        + [pltpu.VMEM((PACKED, CHAN), BF16)] * 6
         + [
             pltpu.VMEM((HEADS * (2 * WT - 1), plane), F32),
             pltpu.VMEM((2 * WH - 1, HEADS * (2 * WT - 1), 128), F32),
             pltpu.VMEM((HEADS, 2 * WH - 1, WT, 128), F32),
             pltpu.VMEM((HEADS, 2 * WH - 1, WW, WT, 128), F32),
             pltpu.VMEM((HEADS, TOK, KEYS), F32),
-            pltpu.VMEM((HEADS, TOK, KEYS), F32),
+            pltpu.VMEM((HEADS, TOK, KEYS), BF16),
+            pltpu.VMEM((HEADS, TOK, KEYS), BF16),
             pltpu.SemaphoreType.DMA((3, len(AWAY))),
             pltpu.SemaphoreType.DMA((3, len(AWAY))),
         ],
         compiler_params=pltpu.CompilerParams(
-            collective_id=0, has_side_effects=True, vmem_limit_bytes=48 * 1024 * 1024
+            collective_id=0, has_side_effects=True, vmem_limit_bytes=54 * 1024 * 1024
         ),
         name="window_block",
     )(*operands)

time: 44.8 us -> 34.5 us (0.77); the launches traced: 44.1 us -> 34.3 us
  local copies, waits for them, and re-layouts: 12 us -> 1.54 us
  Pallas kernels: 32 us -> 32.7 us
    unnamed x39 -> x1, local copies, waits for them, and re-layouts: 12 us -> 1.54 us
    pallas_call x1, Pallas kernels: 32 us -> 32.7 us  [shards(): pl.pallas_call(kernel, out_shape=jax.ShapeDtypeStruct((WH * WW, WT, CHAN)...]
where the time goes in v1:
time: 34.5 us; the launch traced here: 34.3 us
  Pallas kernels  32.7 us (95%)
  local copies, waits for them, and re-layouts  1.54 us (4%)
    pallas_call x1, Pallas kernels, shards(): pl.pallas_call(kernel, out_shape=jax.ShapeDtypeStruct((WH * WW, WT, CHAN)...  32.7 us
    unnamed x1, local copies, waits for them, and re-layouts  1.54 us

profile of v1, /device:TPU:32, one launch (start us, length us, event | category | flops | bytes accessed | tf_op | source)
XLA Modules:
  0.0 34.3 jit_solution(5353132560394391541)
XLA Ops:
  0.0 32.7 %window_block.1 = bf16[49,8,128]{2,1,0:T(8,128)(2,1)} custom-call(bf16[49,8,128]{2,1,0:T(8,128)(2,1)} %bitcast.19, bf16[424,392]{1,0:T(8,128)(2,1)} %constant.8.clone.refs_1_, f32[4,2535]{1,0:T(4,128)} %bitcast.21, bf16[392,416]{1,0:T(8,128)(2,1)} %constant.9.clone.refs_3_, f32[1,128]{1,0:T(1,128)} %bitcast.24, f32[1,128]{1,0:T(1,128)} %bitcast.25, ...), custom_call_target="tpu_custom_call" | custom-call | tf_op jit(solution)/shard_map/window_block/pallas_call | solution.py:431
  32.7 1.5 %copy.21 = bf16[8,1,7,7,128]{4,0,3,2,1:T(8,128)(2,1)} copy(bf16[8,1,7,7,128]{4,0,3,2,1:T(8,128)(2,1)} %bitcast.18) | data formatting | bytes 200704

commit v2 on v1

v2 whole, which is shorter than its diff:
```python
import itertools

import jax
import jax.numpy as jnp
import numpy as np
from jax import lax
from jax.experimental import pallas as pl
from jax.experimental.pallas import tpu as pltpu
from jax.sharding import PartitionSpec as P

HEADS = 4
HEAD = 32
CHAN = 128
FF = 512
WT = 8
WH = 7
WW = 7
ST = 4
SH = 3
SW = 3
TCOLS = 4
TROWS = 4
TM = 16
TOK = WT * WH * WW
KEYS = 512
ROWS = 400
CHUNK = 80
TILES = CHUNK // WT

EPSILON = 1e-05
MASKED = -1000000000.0
INV_ROOT_TAU = 0.3989422804014327
ERF_STEP = 0.3275911 * 0.7071067811865476
ERF_TERMS = (0.254829592, -0.284496736, 1.421413741, -1.453152027, 1.061405429)
SCALE = HEAD ** (-0.5)

F32 = jnp.float32
BF16 = jnp.bfloat16
MESH = pl.DeviceIdType.MESH


CUTS = sorted(itertools.product(range(2), range(2), range(2)), reverse=True)
AWAY = CUTS[:-1]
HALVES = (slice(0, 192), slice(192, TOK))


def box(cut, rolled):
    et, er, ec = cut
    if rolled:
        rows, cols, half = (WH - SH if er else 0), (WW - SW if ec else 0), et
    else:
        rows, cols, half = (0 if er else SH), (0 if ec else SW), 1 - et
    return (pl.ds(rows, SH if er else WH - SH), pl.ds(cols, SW if ec else WW - SW), half)


def dot(a, b, dims=((1,), (0,))):
    return lax.dot_general(a, b, (dims, ((), ())), preferred_element_type=F32)


NT = ((1,), (1,))


def row_mean(values):
    return jnp.sum(values, -1, keepdims=True) * (1.0 / CHAN)


def norm_stats(values):
    center = values - row_mean(values)
    inv_std = lax.rsqrt(row_mean(center * center) + EPSILON)
    return center * inv_std, inv_std


def norm_backward(grad_out, normal, inv_std, gain):
    scaled = grad_out * gain
    return inv_std * (scaled - row_mean(scaled) - normal * row_mean(scaled * normal))


def iota(shape, dim):
    return lax.broadcasted_iota(jnp.int32, shape, dim)


def neighbour(sign, cut):
    time_pos = lax.axis_index("tm")
    tile_pos = lax.axis_index("tile")
    row, col = tile_pos // TCOLS, tile_pos % TCOLS
    et, er, ec = cut
    to_time = (time_pos + TM + sign * et) % TM
    to_row = (row + TROWS + sign * er) % TROWS
    to_col = (col + TCOLS + sign * ec) % TCOLS
    return {"tm": to_time, "tile": to_row * TCOLS + to_col}


def exchange(src, dst, send_sems, recv_sems, to_window):
    remote = [
        pltpu.make_async_remote_copy(
            src_ref=src.at[box(cut, not to_window)],
            dst_ref=dst.at[box(cut, to_window)],
            send_sem=send_sems.at[i],
            recv_sem=recv_sems.at[i],
            device_id=neighbour(-1 if to_window else 1, cut),
            device_id_type=MESH,
        )
        for i, cut in enumerate(AWAY)
    ]
    local = pltpu.make_async_copy(
        src.at[box(CUTS[-1], not to_window)],
        dst.at[box(CUTS[-1], to_window)],
        send_sems.at[len(AWAY)],
    )
    return remote, local


def joined(halves):
    halves = halves.astype(F32).reshape(WH * WW, 2, ST, CHAN)
    return jnp.concatenate([halves[:, 0], halves[:, 1]], axis=1).reshape(TOK, CHAN)


def fill_bias(table, slab_ref, spread_ref, skew_ref, bias_ref):
    time_span, row_span, col_span = 2 * WT - 1, 2 * WH - 1, 2 * WW - 1
    plane = row_span * col_span
    for d in range(time_span):
        slab_ref[HEADS * d : HEADS * (d + 1), :] = table[:, d * plane : (d + 1) * plane]
    slabs = slab_ref[...]
    high = slabs.astype(BF16)
    rest = slabs - high.astype(F32)
    middle = rest.astype(BF16)
    low = (rest - middle.astype(F32)).astype(BF16)
    lanes = iota((1, row_span * 128), 1)
    slot = lanes % 128 // WT
    wanted = jnp.where(slot < col_span, lanes // 128 * col_span + (col_span - 1) - slot, -1)
    pick = (iota((plane, row_span * 128), 0) == wanted).astype(F32).astype(BF16)
    spread = (dot(low, pick) + dot(middle, pick)) + dot(high, pick)
    for p in range(row_span):
        spread_ref[p] = spread[:, p * 128 : (p + 1) * 128]
    lane_time = iota((WT, 128), 1) % WT
    first = iota((WT, 128), 1) < 64

    def fill_head(h, _):
        for p in range(row_span):
            skewed = None
            for a in range(WT):
                rows = spread_ref[p, pl.ds((WT - 1 - a) * HEADS + h, WT, stride=HEADS), :]
                skewed = rows if skewed is None else jnp.where(lane_time == a, rows, skewed)
            skew_ref[p] = skewed
        for d in range(row_span):
            one, two = skew_ref[d], skew_ref[max(d - 1, 0)]
            for c in range(WW):
                shift = WT * (WW - 1 - c)
                bias_ref[h, d * WW + c] = jnp.where(
                    first,
                    one if shift == 0 else pltpu.roll(one, 128 - shift, 1),
                    pltpu.roll(two, 64 - shift, 1),
                )
        return _

    lax.fori_loop(0, HEADS, fill_head, 0)


def gelu_parts(pre_act):
    bell = jnp.exp(-0.5 * pre_act * pre_act)
    step = 1.0 / (1.0 + ERF_STEP * jnp.abs(pre_act))
    tail = ERF_TERMS[4]
    for term in ERF_TERMS[3::-1]:
        tail = tail * step + term
    tail = tail * step * (0.5 * bell)
    share = jnp.where(pre_act < 0.0, tail, 1.0 - tail)
    return pre_act * share, share + pre_act * (INV_ROOT_TAU * bell)


def region_classes(row, col, time):
    last_time = lax.axis_index("tm") == TM - 1
    last_row = lax.axis_index("tile") // TCOLS == TROWS - 1
    last_col = lax.axis_index("tile") % TCOLS == TCOLS - 1
    return (
        jnp.where(time >= ST, jnp.where(last_time, 4, 0), 0)
        + jnp.where(row >= WH - SH, jnp.where(last_row, 2, 0), 0)
        + jnp.where(col >= WW - SW, jnp.where(last_col, 1, 0), 0)
    )


def pad_keys(values):
    blocks = values.reshape(WH, WW, WT, CHAN)
    blocks = jnp.concatenate([blocks, jnp.zeros((WH, 1, WT, CHAN), values.dtype)], axis=1)
    blocks = jnp.concatenate([blocks, jnp.zeros((1, 8, WT, CHAN), values.dtype)], axis=0)
    return blocks.reshape(KEYS, CHAN)


def unpad_keys(values):
    return values.reshape(8, 8, WT, CHAN)[:WH, :WW].reshape(TOK, CHAN)


OPERANDS = (
    "table",
    "gain1",
    "shift1",
    "qkv_weight",
    "qkv_bias",
    "proj_weight",
    "proj_bias",
    "gain2",
    "shift2",
    "fc1_weight",
    "fc1_bias",
    "fc2_weight",
    "fc2_bias",
)


def kernel(*refs):
    count = len(OPERANDS)
    clip_ref, goal_ref, *sources = refs[: count + 2]
    out_ref = refs[count + 2]
    held = refs[count + 3 : 2 * count + 3]
    (
        load_sems,
        clip_in,
        goal_in,
        back_out,
        slab_ref,
        spread_ref,
        skew_ref,
        bias_ref,
        scores_ref,
        probs_ref,
        grads_ref,
        queries_ref,
        classes_ref,
        keys_ref,
        barred_ref,
        values_ref,
        mixed_ref,
        mixed_grad_ref,
        toward_ref,
        grad_queries_ref,
        send_sems,
        recv_sems,
    ) = refs[2 * count + 3 :]

    loads = {}

    def load(i):
        name = OPERANDS[i]
        loads[name] = (pltpu.make_async_copy(sources[i], held[i], load_sems.at[i]), held[i])
        loads[name][0].start()

    barrier = pltpu.get_barrier_semaphore()
    for cut in AWAY:
        pl.semaphore_signal(barrier, inc=1, device_id=neighbour(1, cut), device_id_type=MESH)
    clip_copies, clip_local = exchange(clip_ref, clip_in, send_sems.at[0], recv_sems.at[0], True)
    goal_copies, goal_local = exchange(goal_ref, goal_in, send_sems.at[1], recv_sems.at[1], True)
    back_copies, back_local = exchange(back_out, out_ref, send_sems.at[2], recv_sems.at[2], False)
    clip_local.start()
    for i in range(count):
        load(i)
    goal_local.start()

    def operand(name):
        copy, ref = loads[name]
        copy.wait()
        return ref[...]

    pl.semaphore_wait(barrier, len(AWAY))
    for copy in clip_copies:
        copy.start()

    fill_bias(operand("table"), slab_ref, spread_ref, skew_ref, bias_ref)

    lane = iota((1, CHAN), 1)
    spot = lane % HEAD
    head_masks = [lane // HEAD == h for h in range(HEADS)]
    head_lanes = [mask.astype(F32).astype(BF16) for mask in head_masks]
    token = iota((TOK, 1), 0)
    query_class = region_classes(token // (WW * WT), token % (WW * WT) // WT, token % WT)
    classes_ref[...] = jnp.where(query_class == spot, 1.0, 0.0).astype(BF16)
    key = iota((KEYS, 1), 0)
    key_row, key_col = key // 64, key % 64 // WT
    key_class = region_classes(key_row, key_col, key % WT)
    key_class = jnp.where((key_row < WH) & (key_col < WW), key_class, 8)
    barred_ref[...] = jnp.where((key_class != spot) & (spot < 8), MASKED, 0.0).astype(BF16)

    gain1 = operand("gain1")
    shift1 = operand("shift1")
    qkv_weight = operand("qkv_weight")
    qkv_bias = operand("qkv_bias")
    query_weight_across = qkv_weight[:, :CHAN].T
    query_bias_across = jnp.broadcast_to(qkv_bias[0:1], (CHAN, CHAN)).T[:, 0:1]
    for copy in clip_copies:
        copy.wait_recv()
    clip_local.wait()
    frames = joined(clip_in[...])
    normal1, inv_std1 = norm_stats(frames)
    normed1 = (normal1 * gain1 + shift1).astype(BF16)
    projected = dot(normed1, qkv_weight)
    queries_ref[...] = ((projected[:, :CHAN] + qkv_bias[0:1]) * SCALE).astype(BF16)
    keys_ref[...] = pad_keys(projected[:, CHAN : 2 * CHAN] + qkv_bias[1:2]).astype(BF16)
    values_ref[...] = pad_keys(projected[:, 2 * CHAN :] + qkv_bias[2:3]).astype(BF16)

    for copy in goal_copies:
        copy.start()

    def score(h):
        mine, spare = head_lanes[h], head_lanes[(h + 1) % HEADS]
        head_queries = queries_ref[...] * mine + classes_ref[...] * spare
        head_keys = keys_ref[...] * mine + barred_ref[...] * spare
        scores_ref[h, 0:TOK, :] = dot(head_queries, head_keys, NT)

    def weigh(h):
        for chunk in range(ROWS // CHUNK):
            span = pl.ds(chunk * CHUNK, CHUNK)
            bias = [
                bias_ref[h, pl.ds(chunk * TILES + 42 - 14 * m, TILES)].reshape(CHUNK, 128)
                for m in range(4)
            ]
            scores = scores_ref[h, span, :] + jnp.concatenate(bias, axis=1)
            exponent = jnp.exp(scores - jnp.max(scores, -1, keepdims=True))
            probs_ref[h, span, :] = exponent.astype(BF16)

    def mix(h):
        ones = jnp.broadcast_to(head_lanes[h], (KEYS, CHAN))
        sides = jnp.concatenate([values_ref[...] * head_lanes[h], ones], axis=1)
        part = dot(probs_ref[h, 0:TOK, :], sides)
        mixed_ref[...] = part if h == 0 else mixed_ref[...] + part

    score(0)
    for h in range(HEADS):
        if h + 1 < HEADS:
            score(h + 1)
        if h > 0:
            mix(h - 1)
        weigh(h)
    queries_across = dot(query_weight_across, normed1, NT) + query_bias_across
    queries_across = (queries_across * SCALE).astype(BF16)
    mix(HEADS - 1)

    proj_weight = operand("proj_weight")
    proj_bias = operand("proj_bias")
    gain2 = operand("gain2")
    shift2 = operand("shift2")
    fc1_weight = operand("fc1_weight")
    fc1_bias = operand("fc1_bias")
    fc2_weight = operand("fc2_weight")
    fc2_bias = operand("fc2_bias")
    inv_total = 1.0 / mixed_ref[:, CHAN:]
    mixed = mixed_ref[:, :CHAN] * inv_total
    mixed_low = mixed.astype(BF16)
    branch = [(dot(mixed_low[part], proj_weight) + proj_bias).astype(BF16) for part in HALVES]
    ys = [frames[part] + branch[i].astype(F32) for i, part in enumerate(HALVES)]
    stats2 = [norm_stats(y) for y in ys]
    for i, part in enumerate(HALVES):
        normed2 = (stats2[i][0] * gain2 + shift2).astype(BF16)
        scores_ref[0, part, :] = dot(normed2, fc1_weight) + fc1_bias
    inv_total_across = inv_total.T
    for copy in goal_copies:
        copy.wait_recv()
    goal_local.wait()
    goal = joined(goal_in[...])
    grad_out = []
    for i, part in enumerate(HALVES):
        active, slope = gelu_parts(scores_ref[0, part, :])
        scores_ref[1, part, :] = slope
        grad_out.append(ys[i] + dot(active.astype(BF16), fc2_weight) + (fc2_bias - goal[part]))
    grad_pre = [
        (dot(grad_out[i].astype(BF16), fc2_weight, NT) * scores_ref[1, part, :]).astype(BF16)
        for i, part in enumerate(HALVES)
    ]
    grad_norm2 = [dot(grad, fc1_weight, NT) for grad in grad_pre]
    grad_ys = jnp.concatenate(
        [grad_out[i] + norm_backward(grad_norm2[i], *stats2[i], gain2) for i in range(2)], axis=0
    )

    grad_low = grad_ys.astype(BF16)
    grad_mixed = (dot(grad_low, proj_weight, NT) * inv_total).astype(BF16)
    grad_mixed_across = (dot(proj_weight, grad_low, NT) * inv_total_across).astype(BF16)
    mixed_grad_ref[...] = grad_mixed
    toward_ref[0:TOK, :] = grad_mixed.astype(F32) * mixed

    def score_grad(h):
        scores_ref[h, 0:TOK, :] = dot(mixed_grad_ref[...] * head_lanes[h], values_ref[...], NT)

    def weigh_grad(h):
        for chunk in range(ROWS // CHUNK):
            span = pl.ds(chunk * CHUNK, CHUNK)
            own = jnp.where(head_masks[h], toward_ref[span, :], 0.0)
            delta = jnp.sum(own, -1, keepdims=True)
            probs = probs_ref[h, span, :].astype(F32)
            grads_ref[h, span, :] = (probs * (scores_ref[h, span, :] - delta)).astype(BF16)

    def value_grad(h):
        rows = slice(h * HEAD, (h + 1) * HEAD)
        return dot(grad_mixed_across[rows], probs_ref[h, 0:TOK, :]).astype(BF16)

    def key_grad(h):
        rows = slice(h * HEAD, (h + 1) * HEAD)
        return dot(queries_across[rows], grads_ref[h, 0:TOK, :]).astype(BF16)

    def query_grad(h):
        part = dot(grads_ref[h, 0:TOK, :], keys_ref[...] * head_lanes[h])
        grad_queries_ref[...] = part if h == 0 else grad_queries_ref[...] + part

    grad_values = [None] * HEADS
    grad_keys = [None] * HEADS
    score_grad(0)
    for h in range(HEADS):
        if h + 1 < HEADS:
            score_grad(h + 1)
        grad_values[h] = value_grad(h)
        if h > 0:
            query_grad(h - 1)
            grad_keys[h - 1] = key_grad(h - 1)
        weigh_grad(h)
    grad_keys[HEADS - 1] = key_grad(HEADS - 1)
    query_grad(HEADS - 1)

    across = jnp.concatenate(grad_keys + grad_values, axis=0)
    grad_normed = unpad_keys(dot(qkv_weight[:, CHAN:], across).T)
    grad_queries = (grad_queries_ref[...] * SCALE).astype(BF16)
    grad_normed = grad_normed + dot(grad_queries, qkv_weight[:, :CHAN], NT)
    grad_normed = grad_normed.astype(BF16).astype(F32)
    result = grad_ys + norm_backward(grad_normed, normal1, inv_std1, gain1)

    result = result.reshape(WH, WW, WT, CHAN)
    back_out[:, :, 0] = result[:, :, :ST].astype(BF16)
    back_out[:, :, 1] = result[:, :, ST:].astype(BF16)
    for copy in back_copies:
        copy.start()
    back_local.start()
    for copy in back_copies:
        copy.wait_recv()
    back_local.wait()
    for copy in clip_copies + goal_copies + back_copies:
        copy.wait_send()


def shards(
    clip_tokens,
    target,
    norm1_gain,
    norm1_bias,
    qkv_weight,
    qkv_bias,
    bias_table,
    proj_weight,
    proj_bias,
    norm2_gain,
    norm2_bias,
    fc1_weight,
    fc1_bias,
    fc2_weight,
    fc2_bias,
):
    def by_place(tokens):
        return jnp.transpose(tokens, (1, 2, 3, 0, 4)).reshape(WH, WW, 2, ST, CHAN)

    named = {
        "table": bias_table.T,
        "gain1": norm1_gain.reshape(1, -1),
        "shift1": norm1_bias.reshape(1, -1),
        "qkv_weight": qkv_weight,
        "qkv_bias": qkv_bias.reshape(3, -1),
        "proj_weight": proj_weight,
        "proj_bias": proj_bias.reshape(1, -1),
        "gain2": norm2_gain.reshape(1, -1),
        "shift2": norm2_bias.reshape(1, -1),
        "fc1_weight": fc1_weight,
        "fc1_bias": fc1_bias.reshape(1, -1),
        "fc2_weight": fc2_weight,
        "fc2_bias": fc2_bias.reshape(1, -1),
    }
    operands = [named[name] for name in OPERANDS]
    inputs = [by_place(clip_tokens), by_place(target)] + operands
    plane = (2 * WH - 1) * (2 * WW - 1)
    out = pl.pallas_call(
        kernel,
        out_shape=pltpu.VMEM((WH, WW, 2, ST, CHAN), BF16),
        in_specs=[pl.BlockSpec(memory_space=pltpu.HBM)] * len(inputs),
        out_specs=pl.BlockSpec(memory_space=pltpu.VMEM),
        scratch_shapes=[pltpu.VMEM(x.shape, x.dtype) for x in operands]
        + [pltpu.SemaphoreType.DMA((len(operands),))]
        + [pltpu.VMEM((WH, WW, 2, ST, CHAN), BF16)] * 3
        + [
            pltpu.VMEM((HEADS * (2 * WT - 1), plane), F32),
            pltpu.VMEM((2 * WH - 1, HEADS * (2 * WT - 1), 128), F32),
            pltpu.VMEM((2 * WH - 1, WT, 128), F32),
            pltpu.VMEM((HEADS, (2 * WH - 1) * WW + 1, WT, 128), F32),
            pltpu.VMEM((HEADS, ROWS, KEYS), F32),
            pltpu.VMEM((HEADS, ROWS, KEYS), BF16),
            pltpu.VMEM((HEADS, ROWS, KEYS), BF16),
            pltpu.VMEM((TOK, CHAN), BF16),
            pltpu.VMEM((TOK, CHAN), BF16),
            pltpu.VMEM((KEYS, CHAN), BF16),
            pltpu.VMEM((KEYS, CHAN), BF16),
            pltpu.VMEM((KEYS, CHAN), BF16),
            pltpu.VMEM((TOK, 2 * CHAN), F32),
            pltpu.VMEM((TOK, CHAN), BF16),
            pltpu.VMEM((ROWS, CHAN), F32),
            pltpu.VMEM((TOK, CHAN), F32),
            pltpu.SemaphoreType.DMA((3, len(CUTS))),
            pltpu.SemaphoreType.DMA((3, len(AWAY))),
        ],
        compiler_params=pltpu.CompilerParams(
            collective_id=0, has_side_effects=True, vmem_limit_bytes=40 * 1024 * 1024
        ),
        name="window_block",
    )(*[pltpu.with_memory_space_constraint(x, pltpu.HBM) for x in inputs])
    return jnp.transpose(out.reshape(1, WH, WW, WT, CHAN), (3, 0, 1, 2, 4))


def solution(mesh):
    return jax.shard_map(
        shards,
        mesh=mesh,
        in_specs=(P("tm", "tile", None, None, None),) * 2 + (P(),) * 13,
        out_specs=P("tm", "tile", None, None, None),
        check_vma=False,
    )
```

time: 34.5 us -> 31.9 us (0.925)
  Pallas kernels: 32.7 us -> 31.2 us
  local copies, waits for them, and re-layouts: 1.54 us -> 0.64 us
    pallas_call x1, Pallas kernels: 32.7 us -> 31.2 us  [shards(): pl.pallas_call(kernel, out_shape=pltpu.VMEM((WH, WW, 2, ST, CHAN), BF16),...]
    unnamed x1, local copies, waits for them, and re-layouts: 1.54 us -> 0.64 us
where the time goes in v2:
time: 31.9 us; the launch traced here: 31.8 us
  Pallas kernels  31.2 us (98%)
  local copies, waits for them, and re-layouts  0.64 us (2%)
    pallas_call x1, Pallas kernels, shards(): pl.pallas_call(kernel, out_shape=pltpu.VMEM((WH, WW, 2, ST, CHAN), BF16),...  31.2 us
    unnamed x1, local copies, waits for them, and re-layouts  0.64 us

profile of v2, /device:TPU:32, one launch (start us, length us, event | category | flops | bytes accessed | tf_op | source)
XLA Modules:
  0.0 31.8 jit_solution(3229285884766822599)
XLA Ops:
  0.0 31.2 %window_block.1 = bf16[7,7,2,4,128]{4,3,2,1,0:T(4,128)(2,1)S(1)} custom-call(bf16[7,7,2,4,128]{4,3,2,1,0:T(4,128)(2,1)} %bitcast.19, bf16[7,7,2,4,128]{4,3,2,1,0:T(4,128)(2,1)} %bitcast.20, f32[4,2535]{1,0:T(4,128)} %bitcast.21, f32[1,128]{1,0:T(1,128)} %bitcast.24, f32[1,128]{1,0:T(1,128)} %bitcast.25, bf16[128,384]{1,0:T(8,128)(2,1)} %refs_5_.1, ...), custom_call_target="tpu_custom_call" | custom-call | tf_op jit(solution)/shard_map/window_block/pallas_call | solution.py:472
  31.2 0.6 %copy.17 = bf16[8,1,7,7,128]{4,0,3,2,1:T(8,128)(2,1)} copy(bf16[8,1,7,7,128]{4,0,3,2,1:T(8,128)(2,1)S(1)} %bitcast.18) | data formatting | bytes 200704

commit v3 on v2

--- a/solution.py
+++ b/solution.py
@@ -33,6 +33,7 @@
 ERF_STEP = 0.3275911 * 0.7071067811865476
 ERF_TERMS = (0.254829592, -0.284496736, 1.421413741, -1.453152027, 1.061405429)
 SCALE = HEAD ** (-0.5)
+LOG2E = 1.4426950408889634
 
 F32 = jnp.float32
 BF16 = jnp.bfloat16
@@ -42,6 +43,7 @@
 CUTS = sorted(itertools.product(range(2), range(2), range(2)), reverse=True)
 AWAY = CUTS[:-1]
 HALVES = (slice(0, 192), slice(192, TOK))
+QUARTERS = (slice(0, 96), slice(96, 192), slice(192, 288), slice(288, TOK))
 
 
 def box(cut, rolled):
@@ -115,12 +117,12 @@
     return jnp.concatenate([halves[:, 0], halves[:, 1]], axis=1).reshape(TOK, CHAN)
 
 
-def fill_bias(table, slab_ref, spread_ref, skew_ref, bias_ref):
+def spread_bias(table, slab_ref, spread_ref):
     time_span, row_span, col_span = 2 * WT - 1, 2 * WH - 1, 2 * WW - 1
     plane = row_span * col_span
     for d in range(time_span):
         slab_ref[HEADS * d : HEADS * (d + 1), :] = table[:, d * plane : (d + 1) * plane]
-    slabs = slab_ref[...]
+    slabs = slab_ref[...] * LOG2E
     high = slabs.astype(BF16)
     rest = slabs - high.astype(F32)
     middle = rest.astype(BF16)
@@ -132,6 +134,10 @@
     spread = (dot(low, pick) + dot(middle, pick)) + dot(high, pick)
     for p in range(row_span):
         spread_ref[p] = spread[:, p * 128 : (p + 1) * 128]
+
+
+def fill_bias(spread_ref, skew_ref, bias_ref):
+    row_span = 2 * WH - 1
     lane_time = iota((WT, 128), 1) % WT
     first = iota((WT, 128), 1) < 64
 
@@ -157,7 +163,7 @@
 
 
 def gelu_parts(pre_act):
-    bell = jnp.exp(-0.5 * pre_act * pre_act)
+    bell = jnp.exp2((-0.5 * LOG2E) * pre_act * pre_act)
     step = 1.0 / (1.0 + ERF_STEP * jnp.abs(pre_act))
     tail = ERF_TERMS[4]
     for term in ERF_TERMS[3::-1]:
@@ -263,7 +269,12 @@
     for copy in clip_copies:
         copy.start()
 
-    fill_bias(operand("table"), slab_ref, spread_ref, skew_ref, bias_ref)
+    spread_bias(operand("table"), slab_ref, spread_ref)
+    for copy in clip_copies:
+        copy.wait_send()
+    for copy in goal_copies:
+        copy.start()
+    fill_bias(spread_ref, skew_ref, bias_ref)
 
     lane = iota((1, CHAN), 1)
     spot = lane % HEAD
@@ -284,19 +295,24 @@
     qkv_bias = operand("qkv_bias")
     query_weight_across = qkv_weight[:, :CHAN].T
     query_bias_across = jnp.broadcast_to(qkv_bias[0:1], (CHAN, CHAN)).T[:, 0:1]
+    proj_weight = operand("proj_weight")
+    proj_bias = operand("proj_bias")
+    gain2 = operand("gain2")
+    shift2 = operand("shift2")
+    fc1_weight = operand("fc1_weight")
+    fc1_bias = operand("fc1_bias")
+    fc2_weight = operand("fc2_weight")
+    fc2_bias = operand("fc2_bias")
     for copy in clip_copies:
         copy.wait_recv()
     clip_local.wait()
     frames = joined(clip_in[...])
     normal1, inv_std1 = norm_stats(frames)
     normed1 = (normal1 * gain1 + shift1).astype(BF16)
-    projected = dot(normed1, qkv_weight)
-    queries_ref[...] = ((projected[:, :CHAN] + qkv_bias[0:1]) * SCALE).astype(BF16)
+    projected = jnp.concatenate([dot(normed1[part], qkv_weight) for part in HALVES], axis=0)
+    queries_ref[...] = ((projected[:, :CHAN] + qkv_bias[0:1]) * (SCALE * LOG2E)).astype(BF16)
     keys_ref[...] = pad_keys(projected[:, CHAN : 2 * CHAN] + qkv_bias[1:2]).astype(BF16)
     values_ref[...] = pad_keys(projected[:, 2 * CHAN :] + qkv_bias[2:3]).astype(BF16)
-
-    for copy in goal_copies:
-        copy.start()
 
     def score(h):
         mine, spare = head_lanes[h], head_lanes[(h + 1) % HEADS]
@@ -312,7 +328,7 @@
                 for m in range(4)
             ]
             scores = scores_ref[h, span, :] + jnp.concatenate(bias, axis=1)
-            exponent = jnp.exp(scores - jnp.max(scores, -1, keepdims=True))
+            exponent = jnp.exp2(scores - jnp.max(scores, -1, keepdims=True))
             probs_ref[h, span, :] = exponent.astype(BF16)
 
     def mix(h):
@@ -332,40 +348,33 @@
     queries_across = (queries_across * SCALE).astype(BF16)
     mix(HEADS - 1)
 
-    proj_weight = operand("proj_weight")
-    proj_bias = operand("proj_bias")
-    gain2 = operand("gain2")
-    shift2 = operand("shift2")
-    fc1_weight = operand("fc1_weight")
-    fc1_bias = operand("fc1_bias")
-    fc2_weight = operand("fc2_weight")
-    fc2_bias = operand("fc2_bias")
     inv_total = 1.0 / mixed_ref[:, CHAN:]
     mixed = mixed_ref[:, :CHAN] * inv_total
     mixed_low = mixed.astype(BF16)
-    branch = [(dot(mixed_low[part], proj_weight) + proj_bias).astype(BF16) for part in HALVES]
-    ys = [frames[part] + branch[i].astype(F32) for i, part in enumerate(HALVES)]
+    branch = [(dot(mixed_low[part], proj_weight) + proj_bias).astype(BF16) for part in QUARTERS]
+    ys = [frames[part] + branch[i].astype(F32) for i, part in enumerate(QUARTERS)]
     stats2 = [norm_stats(y) for y in ys]
-    for i, part in enumerate(HALVES):
+    for i, part in enumerate(QUARTERS):
         normed2 = (stats2[i][0] * gain2 + shift2).astype(BF16)
         scores_ref[0, part, :] = dot(normed2, fc1_weight) + fc1_bias
     inv_total_across = inv_total.T
+    outputs = []
+    for i, part in enumerate(QUARTERS):
+        active, slope = gelu_parts(scores_ref[0, part, :])
+        scores_ref[1, part, :] = slope
+        outputs.append(ys[i] + dot(active.astype(BF16), fc2_weight) + fc2_bias)
     for copy in goal_copies:
         copy.wait_recv()
     goal_local.wait()
     goal = joined(goal_in[...])
-    grad_out = []
-    for i, part in enumerate(HALVES):
-        active, slope = gelu_parts(scores_ref[0, part, :])
-        scores_ref[1, part, :] = slope
-        grad_out.append(ys[i] + dot(active.astype(BF16), fc2_weight) + (fc2_bias - goal[part]))
+    grad_out = [outputs[i] - goal[part] for i, part in enumerate(QUARTERS)]
     grad_pre = [
         (dot(grad_out[i].astype(BF16), fc2_weight, NT) * scores_ref[1, part, :]).astype(BF16)
-        for i, part in enumerate(HALVES)
+        for i, part in enumerate(QUARTERS)
     ]
     grad_norm2 = [dot(grad, fc1_weight, NT) for grad in grad_pre]
     grad_ys = jnp.concatenate(
-        [grad_out[i] + norm_backward(grad_norm2[i], *stats2[i], gain2) for i in range(2)], axis=0
+        [grad_out[i] + norm_backward(grad_norm2[i], *stats2[i], gain2) for i in range(4)], axis=0
     )
 
     grad_low = grad_ys.astype(BF16)
@@ -382,8 +391,8 @@
             span = pl.ds(chunk * CHUNK, CHUNK)
             own = jnp.where(head_masks[h], toward_ref[span, :], 0.0)
             delta = jnp.sum(own, -1, keepdims=True)
-            probs = probs_ref[h, span, :].astype(F32)
-            grads_ref[h, span, :] = (probs * (scores_ref[h, span, :] - delta)).astype(BF16)
+            excess = (scores_ref[h, span, :] - delta).astype(BF16)
+            grads_ref[h, span, :] = probs_ref[h, span, :] * excess
 
     def value_grad(h):
         rows = slice(h * HEAD, (h + 1) * HEAD)
@@ -414,20 +423,23 @@
     across = jnp.concatenate(grad_keys + grad_values, axis=0)
     grad_normed = unpad_keys(dot(qkv_weight[:, CHAN:], across).T)
     grad_queries = (grad_queries_ref[...] * SCALE).astype(BF16)
-    grad_normed = grad_normed + dot(grad_queries, qkv_weight[:, :CHAN], NT)
-    grad_normed = grad_normed.astype(BF16).astype(F32)
-    result = grad_ys + norm_backward(grad_normed, normal1, inv_std1, gain1)
-
-    result = result.reshape(WH, WW, WT, CHAN)
-    back_out[:, :, 0] = result[:, :, :ST].astype(BF16)
-    back_out[:, :, 1] = result[:, :, ST:].astype(BF16)
-    for copy in back_copies:
-        copy.start()
-    back_local.start()
+    for group, rows in enumerate((range(0, WH - SH), range(WH - SH, WH))):
+        part = slice(rows.start * WW * WT, rows.stop * WW * WT)
+        total = grad_normed[part] + dot(grad_queries[part], qkv_weight[:, :CHAN], NT)
+        total = total.astype(BF16).astype(F32)
+        result = grad_ys[part] + norm_backward(total, normal1[part], inv_std1[part], gain1)
+        result = result.reshape(len(rows), WW, WT, CHAN)
+        back_out[rows.start : rows.stop, :, 0] = result[:, :, :ST].astype(BF16)
+        back_out[rows.start : rows.stop, :, 1] = result[:, :, ST:].astype(BF16)
+        for cut, copy in zip(AWAY, back_copies):
+            if cut[1] == group:
+                copy.start()
+        if group == 0:
+            back_local.start()
     for copy in back_copies:
         copy.wait_recv()
     back_local.wait()
-    for copy in clip_copies + goal_copies + back_copies:
+    for copy in goal_copies + back_copies:
         copy.wait_send()
 
 

time: 31.9 us -> 30.6 us (0.959)
  Pallas kernels: 31.2 us -> 29.9 us
    pallas_call x1, Pallas kernels: 31.2 us -> 29.9 us  [shards(): pl.pallas_call(kernel, out_shape=pltpu.VMEM((WH, WW, 2, ST, CHAN), BF16),...]
where the time goes in v3:
time: 30.6 us; the launch traced here: 30.5 us
  Pallas kernels  29.9 us (98%)
  local copies, waits for them, and re-layouts  0.64 us (2%)
    pallas_call x1, Pallas kernels, shards(): pl.pallas_call(kernel, out_shape=pltpu.VMEM((WH, WW, 2, ST, CHAN), BF16),...  29.9 us
    unnamed x1, local copies, waits for them, and re-layouts  0.64 us

profile of v3, /device:TPU:32, one launch (start us, length us, event | category | flops | bytes accessed | tf_op | source)
XLA Modules:
  0.0 30.5 jit_solution(14713711294120589695)
XLA Ops:
  0.0 29.9 %window_block.1 = bf16[7,7,2,4,128]{4,3,2,1,0:T(4,128)(2,1)S(1)} custom-call(bf16[7,7,2,4,128]{4,3,2,1,0:T(4,128)(2,1)} %bitcast.19, bf16[7,7,2,4,128]{4,3,2,1,0:T(4,128)(2,1)} %bitcast.20, f32[4,2535]{1,0:T(4,128)} %bitcast.21, f32[1,128]{1,0:T(1,128)} %bitcast.24, f32[1,128]{1,0:T(1,128)} %bitcast.25, bf16[128,384]{1,0:T(8,128)(2,1)} %refs_5_.1, ...), custom_call_target="tpu_custom_call" | custom-call | tf_op jit(solution)/shard_map/window_block/pallas_call | solution.py:484
  29.9 0.6 %copy.17 = bf16[8,1,7,7,128]{4,0,3,2,1:T(8,128)(2,1)} copy(bf16[8,1,7,7,128]{4,0,3,2,1:T(8,128)(2,1)S(1)} %bitcast.18) | data formatting | bytes 200704

commit v4 on v3

--- a/solution.py
+++ b/solution.py
@@ -42,6 +42,8 @@
 
 CUTS = sorted(itertools.product(range(2), range(2), range(2)), reverse=True)
 AWAY = CUTS[:-1]
+IN_TIME = [cut for cut in AWAY if cut[0]]
+RELAY = TM // 2 - 1
 HALVES = (slice(0, 192), slice(192, TOK))
 QUARTERS = (slice(0, 96), slice(96, 192), slice(192, 288), slice(288, TOK))
 
@@ -81,35 +83,130 @@
     return lax.broadcasted_iota(jnp.int32, shape, dim)
 
 
+def position():
+    tile_pos = lax.axis_index("tile")
+    return lax.axis_index("tm"), tile_pos // TCOLS, tile_pos % TCOLS
+
+
+def device(time, row, col):
+    return {"tm": time, "tile": row * TCOLS + col}
+
+
 def neighbour(sign, cut):
-    time_pos = lax.axis_index("tm")
-    tile_pos = lax.axis_index("tile")
-    row, col = tile_pos // TCOLS, tile_pos % TCOLS
+    time, row, col = position()
     et, er, ec = cut
-    to_time = (time_pos + TM + sign * et) % TM
-    to_row = (row + TROWS + sign * er) % TROWS
-    to_col = (col + TCOLS + sign * ec) % TCOLS
-    return {"tm": to_time, "tile": to_row * TCOLS + to_col}
-
-
-def exchange(src, dst, send_sems, recv_sems, to_window):
-    remote = [
-        pltpu.make_async_remote_copy(
-            src_ref=src.at[box(cut, not to_window)],
-            dst_ref=dst.at[box(cut, to_window)],
-            send_sem=send_sems.at[i],
-            recv_sem=recv_sems.at[i],
-            device_id=neighbour(-1 if to_window else 1, cut),
+    return (
+        (time + TM + sign * et) % TM,
+        (row + TROWS + sign * er) % TROWS,
+        (col + TCOLS + sign * ec) % TCOLS,
+    )
+
+
+def opposite(row):
+    return (row + TROWS // 2) % TROWS
+
+
+def sender(cut):
+    time, row, col = neighbour(1, cut)
+    if cut[0]:
+        last = position()[0] == TM - 1
+        time, row = jnp.where(last, RELAY, time), jnp.where(last, opposite(row), row)
+    return device(time, row, col)
+
+
+class Exchange:
+    def __init__(self, src, dst, sems, to_window, relay=None):
+        send_sems, recv_sems = sems[:2]
+        self.to_window = to_window
+        self.remote = {
+            cut: pltpu.make_async_remote_copy(
+                src_ref=src.at[box(cut, not to_window)],
+                dst_ref=dst.at[box(cut, to_window)],
+                send_sem=send_sems.at[i],
+                recv_sem=recv_sems.at[i],
+                device_id=device(*neighbour(-1 if to_window else 1, cut)),
+                device_id_type=MESH,
+            )
+            for i, cut in enumerate(AWAY)
+        }
+        self.local = pltpu.make_async_copy(
+            src.at[box(CUTS[-1], not to_window)],
+            dst.at[box(CUTS[-1], to_window)],
+            send_sems.at[len(AWAY)],
+        )
+        if not to_window:
+            return
+        relay_sems, onward_sems = sems[2:]
+        self.time, row, col = position()
+        self.hand_over = pltpu.make_async_remote_copy(
+            src_ref=src.at[:, :, 0],
+            dst_ref=relay,
+            send_sem=relay_sems.at[0],
+            recv_sem=relay_sems.at[1],
+            device_id=device(RELAY, opposite(row), col),
             device_id_type=MESH,
         )
-        for i, cut in enumerate(AWAY)
-    ]
-    local = pltpu.make_async_copy(
-        src.at[box(CUTS[-1], not to_window)],
-        dst.at[box(CUTS[-1], to_window)],
-        send_sems.at[len(AWAY)],
-    )
-    return remote, local
+        self.onward = [
+            pltpu.make_async_remote_copy(
+                src_ref=relay.at[box(cut, False)[:2]],
+                dst_ref=dst.at[box(cut, True)],
+                send_sem=onward_sems.at[i],
+                recv_sem=recv_sems.at[AWAY.index(cut)],
+                device_id=device(
+                    TM - 1,
+                    (opposite(row) + TROWS - cut[1]) % TROWS,
+                    (col + TCOLS - cut[2]) % TCOLS,
+                ),
+                device_id_type=MESH,
+            )
+            for i, cut in enumerate(IN_TIME)
+        ]
+
+    def start(self):
+        @pl.when(self.time == 0)
+        def _():
+            self.hand_over.start()
+
+        @pl.when(self.time != 0)
+        def _():
+            for cut in IN_TIME:
+                self.remote[cut].start()
+
+        for cut in AWAY:
+            if not cut[0]:
+                self.remote[cut].start()
+
+    def pass_on(self):
+        @pl.when(self.time == RELAY)
+        def _():
+            self.hand_over.wait_recv()
+            for copy in self.onward:
+                copy.start()
+
+    def wait_sent(self):
+        @pl.when(self.time == 0)
+        def _():
+            self.hand_over.wait_send()
+
+        @pl.when(self.time != 0)
+        def _():
+            for cut in IN_TIME:
+                self.remote[cut].wait_send()
+
+        for cut in AWAY:
+            if not cut[0]:
+                self.remote[cut].wait_send()
+
+    def wait_passed_on(self):
+        @pl.when(self.time == RELAY)
+        def _():
+            for copy in self.onward:
+                copy.wait_send()
+
+    def wait_received(self):
+        for cut in AWAY:
+            self.remote[cut].wait_recv()
+        self.local.wait()
 
 
 def joined(halves):
@@ -222,6 +319,8 @@
         clip_in,
         goal_in,
         back_out,
+        clip_relay,
+        goal_relay,
         slab_ref,
         spread_ref,
         skew_ref,
@@ -240,6 +339,8 @@
         grad_queries_ref,
         send_sems,
         recv_sems,
+        relay_sems,
+        onward_sems,
     ) = refs[2 * count + 3 :]
 
     loads = {}
@@ -249,32 +350,42 @@
         loads[name] = (pltpu.make_async_copy(sources[i], held[i], load_sems.at[i]), held[i])
         loads[name][0].start()
 
+    time_pos, row_pos, col_pos = position()
     barrier = pltpu.get_barrier_semaphore()
     for cut in AWAY:
-        pl.semaphore_signal(barrier, inc=1, device_id=neighbour(1, cut), device_id_type=MESH)
-    clip_copies, clip_local = exchange(clip_ref, clip_in, send_sems.at[0], recv_sems.at[0], True)
-    goal_copies, goal_local = exchange(goal_ref, goal_in, send_sems.at[1], recv_sems.at[1], True)
-    back_copies, back_local = exchange(back_out, out_ref, send_sems.at[2], recv_sems.at[2], False)
-    clip_local.start()
+        pl.semaphore_signal(barrier, inc=1, device_id=sender(cut), device_id_type=MESH)
+
+    @pl.when(time_pos == RELAY)
+    def _():
+        first_block = device(0, opposite(row_pos), col_pos)
+        pl.semaphore_signal(barrier, inc=1, device_id=first_block, device_id_type=MESH)
+
+    def sems_of(k):
+        return send_sems.at[k], recv_sems.at[k], relay_sems.at[k], onward_sems.at[k]
+
+    clip = Exchange(clip_ref, clip_in, sems_of(0), True, clip_relay)
+    goal = Exchange(goal_ref, goal_in, sems_of(1), True, goal_relay)
+    back = Exchange(back_out, out_ref, (send_sems.at[2], recv_sems.at[2]), False)
+    clip.local.start()
     for i in range(count):
         load(i)
-    goal_local.start()
+    goal.local.start()
 
     def operand(name):
         copy, ref = loads[name]
         copy.wait()
         return ref[...]
 
-    pl.semaphore_wait(barrier, len(AWAY))
-    for copy in clip_copies:
-        copy.start()
-
+    targets = len(AWAY) + jnp.where(time_pos == RELAY, len(IN_TIME), 0)
+    targets = targets - jnp.where(time_pos == 0, len(IN_TIME) - 1, 0)
+    pl.semaphore_wait(barrier, targets)
+    clip.start()
+    clip.pass_on()
     spread_bias(operand("table"), slab_ref, spread_ref)
-    for copy in clip_copies:
-        copy.wait_send()
-    for copy in goal_copies:
-        copy.start()
+    clip.wait_sent()
+    goal.start()
     fill_bias(spread_ref, skew_ref, bias_ref)
+    goal.pass_on()
 
     lane = iota((1, CHAN), 1)
     spot = lane % HEAD
@@ -303,9 +414,7 @@
     fc1_bias = operand("fc1_bias")
     fc2_weight = operand("fc2_weight")
     fc2_bias = operand("fc2_bias")
-    for copy in clip_copies:
-        copy.wait_recv()
-    clip_local.wait()
+    clip.wait_received()
     frames = joined(clip_in[...])
     normal1, inv_std1 = norm_stats(frames)
     normed1 = (normal1 * gain1 + shift1).astype(BF16)
@@ -363,11 +472,9 @@
         active, slope = gelu_parts(scores_ref[0, part, :])
         scores_ref[1, part, :] = slope
         outputs.append(ys[i] + dot(active.astype(BF16), fc2_weight) + fc2_bias)
-    for copy in goal_copies:
-        copy.wait_recv()
-    goal_local.wait()
-    goal = joined(goal_in[...])
-    grad_out = [outputs[i] - goal[part] for i, part in enumerate(QUARTERS)]
+    goal.wait_received()
+    wanted = joined(goal_in[...])
+    grad_out = [outputs[i] - wanted[part] for i, part in enumerate(QUARTERS)]
     grad_pre = [
         (dot(grad_out[i].astype(BF16), fc2_weight, NT) * scores_ref[1, part, :]).astype(BF16)
         for i, part in enumerate(QUARTERS)
@@ -431,16 +538,17 @@
         result = result.reshape(len(rows), WW, WT, CHAN)
         back_out[rows.start : rows.stop, :, 0] = result[:, :, :ST].astype(BF16)
         back_out[rows.start : rows.stop, :, 1] = result[:, :, ST:].astype(BF16)
-        for cut, copy in zip(AWAY, back_copies):
+        for cut in AWAY:
             if cut[1] == group:
-                copy.start()
+                back.remote[cut].start()
         if group == 0:
-            back_local.start()
-    for copy in back_copies:
-        copy.wait_recv()
-    back_local.wait()
-    for copy in goal_copies + back_copies:
-        copy.wait_send()
+            back.local.start()
+    back.wait_received()
+    goal.wait_sent()
+    clip.wait_passed_on()
+    goal.wait_passed_on()
+    for cut in AWAY:
+        back.remote[cut].wait_send()
 
 
 def shards(
@@ -489,6 +597,7 @@
         scratch_shapes=[pltpu.VMEM(x.shape, x.dtype) for x in operands]
         + [pltpu.SemaphoreType.DMA((len(operands),))]
         + [pltpu.VMEM((WH, WW, 2, ST, CHAN), BF16)] * 3
+        + [pltpu.VMEM((WH, WW, ST, CHAN), BF16)] * 2
         + [
             pltpu.VMEM((HEADS * (2 * WT - 1), plane), F32),
             pltpu.VMEM((2 * WH - 1, HEADS * (2 * WT - 1), 128), F32),
@@ -508,6 +617,8 @@
             pltpu.VMEM((TOK, CHAN), F32),
             pltpu.SemaphoreType.DMA((3, len(CUTS))),
             pltpu.SemaphoreType.DMA((3, len(AWAY))),
+            pltpu.SemaphoreType.DMA((2, 2)),
+            pltpu.SemaphoreType.DMA((2, len(IN_TIME))),
         ],
         compiler_params=pltpu.CompilerParams(
             collective_id=0, has_side_effects=True, vmem_limit_bytes=40 * 1024 * 1024

time: 30.6 us -> 28.2 us (0.922)
  Pallas kernels: 29.9 us -> 27.5 us
    pallas_call x1, Pallas kernels: 29.9 us -> 27.5 us  [shards(): pl.pallas_call(kernel, out_shape=pltpu.VMEM((WH, WW, 2, ST, CHAN), BF16),...]
where the time goes in v4:
time: 28.2 us; the launch traced here: 28.1 us
  Pallas kernels  27.5 us (98%)
  local copies, waits for them, and re-layouts  0.64 us (2%)
    pallas_call x1, Pallas kernels, shards(): pl.pallas_call(kernel, out_shape=pltpu.VMEM((WH, WW, 2, ST, CHAN), BF16),...  27.5 us
    unnamed x1, local copies, waits for them, and re-layouts  0.64 us

profile of v4, /device:TPU:32, one launch (start us, length us, event | category | flops | bytes accessed | tf_op | source)
XLA Modules:
  0.0 28.1 jit_solution(1560898120460982651)
XLA Ops:
  0.0 27.5 %window_block.1 = bf16[7,7,2,4,128]{4,3,2,1,0:T(4,128)(2,1)S(1)} custom-call(bf16[7,7,2,4,128]{4,3,2,1,0:T(4,128)(2,1)} %bitcast.19, bf16[7,7,2,4,128]{4,3,2,1,0:T(4,128)(2,1)} %bitcast.20, f32[4,2535]{1,0:T(4,128)} %bitcast.21, f32[1,128]{1,0:T(1,128)} %bitcast.24, f32[1,128]{1,0:T(1,128)} %bitcast.25, bf16[128,384]{1,0:T(8,128)(2,1)} %refs_5_.1, ...), custom_call_target="tpu_custom_call" | custom-call | tf_op jit(solution)/shard_map/window_block/pallas_call | solution.py:592
  27.5 0.6 %copy.17 = bf16[8,1,7,7,128]{4,0,3,2,1:T(8,128)(2,1)} copy(bf16[8,1,7,7,128]{4,0,3,2,1:T(8,128)(2,1)S(1)} %bitcast.18) | data formatting | bytes 200704

commit v5 on v3

--- a/solution.py
+++ b/solution.py
@@ -41,7 +41,7 @@
 
 
 CUTS = sorted(itertools.product(range(2), range(2), range(2)), reverse=True)
-AWAY = CUTS[:-1]
+AWAY, STAYS = CUTS[:-1], CUTS[-1]
 HALVES = (slice(0, 192), slice(192, TOK))
 QUARTERS = (slice(0, 96), slice(96, 192), slice(192, 288), slice(288, TOK))
 
@@ -81,35 +81,72 @@
     return lax.broadcasted_iota(jnp.int32, shape, dim)
 
 
-def neighbour(sign, cut):
-    time_pos = lax.axis_index("tm")
+def position():
     tile_pos = lax.axis_index("tile")
-    row, col = tile_pos // TCOLS, tile_pos % TCOLS
-    et, er, ec = cut
-    to_time = (time_pos + TM + sign * et) % TM
-    to_row = (row + TROWS + sign * er) % TROWS
-    to_col = (col + TCOLS + sign * ec) % TCOLS
-    return {"tm": to_time, "tile": to_row * TCOLS + to_col}
-
-
-def exchange(src, dst, send_sems, recv_sems, to_window):
-    remote = [
-        pltpu.make_async_remote_copy(
-            src_ref=src.at[box(cut, not to_window)],
-            dst_ref=dst.at[box(cut, to_window)],
-            send_sem=send_sems.at[i],
-            recv_sem=recv_sems.at[i],
-            device_id=neighbour(-1 if to_window else 1, cut),
-            device_id_type=MESH,
+    return lax.axis_index("tm"), tile_pos // TCOLS, tile_pos % TCOLS
+
+
+def crosses(time):
+    return time % (TM // 2) == TM // 2 - 1
+
+
+def swapped(time, row):
+    return jnp.where(crosses(time), (row + TROWS // 2) % TROWS, row)
+
+
+def device(time, row, col):
+    return {"tm": time, "tile": row * TCOLS + col}
+
+
+def target(cut):
+    time, row, col = position()
+    time = (time + TM - cut[0]) % TM
+    row = swapped(time, (row + TROWS - cut[1]) % TROWS)
+    return device(time, row, (col + TCOLS - cut[2]) % TCOLS)
+
+
+def source(cut):
+    time, row, col = position()
+    row = swapped(time, row)
+    return device((time + cut[0]) % TM, (row + cut[1]) % TROWS, (col + cut[2]) % TCOLS)
+
+
+class Exchange:
+    def __init__(self, src, dst, send_sems, recv_sems, local_sem, to_window):
+        self.away = crosses(position()[0])
+        self.remote = {
+            cut: pltpu.make_async_remote_copy(
+                src_ref=src.at[box(cut, not to_window)],
+                dst_ref=dst.at[box(cut, to_window)],
+                send_sem=send_sems.at[i],
+                recv_sem=recv_sems.at[i],
+                device_id=target(cut) if to_window else source(cut),
+                device_id_type=MESH,
+            )
+            for i, cut in enumerate(CUTS)
+        }
+        self.local = pltpu.make_async_copy(
+            src.at[box(STAYS, not to_window)], dst.at[box(STAYS, to_window)], local_sem
         )
-        for i, cut in enumerate(AWAY)
-    ]
-    local = pltpu.make_async_copy(
-        src.at[box(CUTS[-1], not to_window)],
-        dst.at[box(CUTS[-1], to_window)],
-        send_sems.at[len(AWAY)],
-    )
-    return remote, local
+
+    def start(self, cuts):
+        for cut in cuts:
+            if cut == STAYS:
+                pl.when(self.away)(self.remote[cut].start)
+                pl.when(jnp.logical_not(self.away))(self.local.start)
+            else:
+                self.remote[cut].start()
+
+    def wait_sent(self):
+        for cut in AWAY:
+            self.remote[cut].wait_send()
+        pl.when(self.away)(self.remote[STAYS].wait_send)
+
+    def wait_received(self):
+        for cut in AWAY:
+            self.remote[cut].wait_recv()
+        pl.when(self.away)(self.remote[STAYS].wait_recv)
+        pl.when(jnp.logical_not(self.away))(self.local.wait)
 
 
 def joined(halves):
@@ -174,9 +211,10 @@
 
 
 def region_classes(row, col, time):
-    last_time = lax.axis_index("tm") == TM - 1
-    last_row = lax.axis_index("tile") // TCOLS == TROWS - 1
-    last_col = lax.axis_index("tile") % TCOLS == TCOLS - 1
+    time_pos, row_pos, col_pos = position()
+    last_time = time_pos == TM - 1
+    last_row = swapped(time_pos, row_pos) == TROWS - 1
+    last_col = col_pos == TCOLS - 1
     return (
         jnp.where(time >= ST, jnp.where(last_time, 4, 0), 0)
         + jnp.where(row >= WH - SH, jnp.where(last_row, 2, 0), 0)
@@ -240,6 +278,7 @@
         grad_queries_ref,
         send_sems,
         recv_sems,
+        local_sems,
     ) = refs[2 * count + 3 :]
 
     loads = {}
@@ -249,31 +288,34 @@
         loads[name] = (pltpu.make_async_copy(sources[i], held[i], load_sems.at[i]), held[i])
         loads[name][0].start()
 
+    away = crosses(position()[0])
     barrier = pltpu.get_barrier_semaphore()
     for cut in AWAY:
-        pl.semaphore_signal(barrier, inc=1, device_id=neighbour(1, cut), device_id_type=MESH)
-    clip_copies, clip_local = exchange(clip_ref, clip_in, send_sems.at[0], recv_sems.at[0], True)
-    goal_copies, goal_local = exchange(goal_ref, goal_in, send_sems.at[1], recv_sems.at[1], True)
-    back_copies, back_local = exchange(back_out, out_ref, send_sems.at[2], recv_sems.at[2], False)
-    clip_local.start()
+        pl.semaphore_signal(barrier, inc=1, device_id=source(cut), device_id_type=MESH)
+
+    @pl.when(away)
+    def _():
+        pl.semaphore_signal(barrier, inc=1, device_id=source(STAYS), device_id_type=MESH)
+
+    clip, goal, back = (
+        Exchange(src, dst, send_sems.at[k], recv_sems.at[k], local_sems.at[k], k < 2)
+        for k, (src, dst) in enumerate(
+            ((clip_ref, clip_in), (goal_ref, goal_in), (back_out, out_ref))
+        )
+    )
     for i in range(count):
         load(i)
-    goal_local.start()
 
     def operand(name):
         copy, ref = loads[name]
         copy.wait()
         return ref[...]
 
-    pl.semaphore_wait(barrier, len(AWAY))
-    for copy in clip_copies:
-        copy.start()
-
+    pl.semaphore_wait(barrier, jnp.where(away, len(CUTS), len(AWAY)))
+    clip.start(CUTS)
     spread_bias(operand("table"), slab_ref, spread_ref)
-    for copy in clip_copies:
-        copy.wait_send()
-    for copy in goal_copies:
-        copy.start()
+    clip.wait_sent()
+    goal.start(CUTS)
     fill_bias(spread_ref, skew_ref, bias_ref)
 
     lane = iota((1, CHAN), 1)
@@ -303,9 +345,7 @@
     fc1_bias = operand("fc1_bias")
     fc2_weight = operand("fc2_weight")
     fc2_bias = operand("fc2_bias")
-    for copy in clip_copies:
-        copy.wait_recv()
-    clip_local.wait()
+    clip.wait_received()
     frames = joined(clip_in[...])
     normal1, inv_std1 = norm_stats(frames)
     normed1 = (normal1 * gain1 + shift1).astype(BF16)
@@ -363,11 +403,9 @@
         active, slope = gelu_parts(scores_ref[0, part, :])
         scores_ref[1, part, :] = slope
         outputs.append(ys[i] + dot(active.astype(BF16), fc2_weight) + fc2_bias)
-    for copy in goal_copies:
-        copy.wait_recv()
-    goal_local.wait()
-    goal = joined(goal_in[...])
-    grad_out = [outputs[i] - goal[part] for i, part in enumerate(QUARTERS)]
+    goal.wait_received()
+    wanted = joined(goal_in[...])
+    grad_out = [outputs[i] - wanted[part] for i, part in enumerate(QUARTERS)]
     grad_pre = [
         (dot(grad_out[i].astype(BF16), fc2_weight, NT) * scores_ref[1, part, :]).astype(BF16)
         for i, part in enumerate(QUARTERS)
@@ -431,16 +469,10 @@
         result = result.reshape(len(rows), WW, WT, CHAN)
         back_out[rows.start : rows.stop, :, 0] = result[:, :, :ST].astype(BF16)
         back_out[rows.start : rows.stop, :, 1] = result[:, :, ST:].astype(BF16)
-        for cut, copy in zip(AWAY, back_copies):
-            if cut[1] == group:
-                copy.start()
-        if group == 0:
-            back_local.start()
-    for copy in back_copies:
-        copy.wait_recv()
-    back_local.wait()
-    for copy in goal_copies + back_copies:
-        copy.wait_send()
+        back.start([cut for cut in CUTS if cut[1] == group])
+    back.wait_received()
+    goal.wait_sent()
+    back.wait_sent()
 
 
 def shards(
@@ -507,7 +539,8 @@
             pltpu.VMEM((ROWS, CHAN), F32),
             pltpu.VMEM((TOK, CHAN), F32),
             pltpu.SemaphoreType.DMA((3, len(CUTS))),
-            pltpu.SemaphoreType.DMA((3, len(AWAY))),
+            pltpu.SemaphoreType.DMA((3, len(CUTS))),
+            pltpu.SemaphoreType.DMA((3,)),
         ],
         compiler_params=pltpu.CompilerParams(
             collective_id=0, has_side_effects=True, vmem_limit_bytes=40 * 1024 * 1024

time: 30.6 us -> 29.2 us (0.954)
  Pallas kernels: 29.9 us -> 28.5 us
    pallas_call x1, Pallas kernels: 29.9 us -> 28.5 us  [shards(): pl.pallas_call(kernel, out_shape=pltpu.VMEM((WH, WW, 2, ST, CHAN), BF16),...]
where the time goes in v5:
time: 29.2 us
  Pallas kernels  28.5 us (98%)
  local copies, waits for them, and re-layouts  0.64 us (2%)
    pallas_call x1, Pallas kernels, shards(): pl.pallas_call(kernel, out_shape=pltpu.VMEM((WH, WW, 2, ST, CHAN), BF16),...  28.5 us
    unnamed x1, local copies, waits for them, and re-layouts  0.64 us

profile of v5, /device:TPU:32, one launch (start us, length us, event | category | flops | bytes accessed | tf_op | source)
XLA Modules:
  0.0 29.2 jit_solution(4638747104332001761)
XLA Ops:
  0.0 28.5 %window_block.1 = bf16[7,7,2,4,128]{4,3,2,1,0:T(4,128)(2,1)S(1)} custom-call(bf16[7,7,2,4,128]{4,3,2,1,0:T(4,128)(2,1)} %bitcast.19, bf16[7,7,2,4,128]{4,3,2,1,0:T(4,128)(2,1)} %bitcast.20, f32[4,2535]{1,0:T(4,128)} %bitcast.21, f32[1,128]{1,0:T(1,128)} %bitcast.24, f32[1,128]{1,0:T(1,128)} %bitcast.25, bf16[128,384]{1,0:T(8,128)(2,1)} %refs_5_.1, ...), custom_call_target="tpu_custom_call" | custom-call | tf_op jit(solution)/shard_map/window_block/pallas_call | solution.py:516
  28.5 0.6 %copy.17 = bf16[8,1,7,7,128]{4,0,3,2,1:T(8,128)(2,1)} copy(bf16[8,1,7,7,128]{4,0,3,2,1:T(8,128)(2,1)S(1)} %bitcast.18) | data formatting | bytes 200704

commit v6 on v5

--- a/solution.py
+++ b/solution.py
@@ -42,6 +42,8 @@
 
 CUTS = sorted(itertools.product(range(2), range(2), range(2)), reverse=True)
 AWAY, STAYS = CUTS[:-1], CUTS[-1]
+IN_TIME = [cut for cut in AWAY if cut[0]]
+RELAY = TM // 2 - 1
 HALVES = (slice(0, 192), slice(192, TOK))
 QUARTERS = (slice(0, 96), slice(96, 192), slice(192, 288), slice(288, TOK))
 
@@ -111,9 +113,18 @@
     return device((time + cut[0]) % TM, (row + cut[1]) % TROWS, (col + cut[2]) % TCOLS)
 
 
+def sender(cut):
+    where = source(cut)
+    if cut[0]:
+        where["tm"] = jnp.where(position()[0] == TM - 1, RELAY, where["tm"])
+    return where
+
+
 class Exchange:
-    def __init__(self, src, dst, send_sems, recv_sems, local_sem, to_window):
-        self.away = crosses(position()[0])
+    def __init__(self, src, dst, sems, to_window, relay=None):
+        send_sems, recv_sems, local_sem = sems[:3]
+        self.time, row, col = position()
+        self.away = crosses(self.time)
         self.remote = {
             cut: pltpu.make_async_remote_copy(
                 src_ref=src.at[box(cut, not to_window)],
@@ -128,8 +139,53 @@
         self.local = pltpu.make_async_copy(
             src.at[box(STAYS, not to_window)], dst.at[box(STAYS, to_window)], local_sem
         )
+        self.relayed = to_window
+        if not to_window:
+            return
+        relay_sems, onward_sems = sems[3:]
+        self.hand_over = pltpu.make_async_remote_copy(
+            src_ref=src.at[:, :, 0],
+            dst_ref=relay,
+            send_sem=relay_sems.at[0],
+            recv_sem=relay_sems.at[1],
+            device_id=device(RELAY, row, col),
+            device_id_type=MESH,
+        )
+        self.onward = [
+            pltpu.make_async_remote_copy(
+                src_ref=relay.at[box(cut, False)[:2]],
+                dst_ref=dst.at[box(cut, True)],
+                send_sem=onward_sems.at[i],
+                recv_sem=recv_sems.at[CUTS.index(cut)],
+                device_id=device(
+                    TM - 1,
+                    swapped(TM - 1, (row + TROWS - cut[1]) % TROWS),
+                    (col + TCOLS - cut[2]) % TCOLS,
+                ),
+                device_id_type=MESH,
+            )
+            for i, cut in enumerate(IN_TIME)
+        ]
+
+    def over_time(self, act):
+        if not self.relayed:
+            for cut in IN_TIME:
+                act(self.remote[cut])
+            return
+
+        @pl.when(self.time == 0)
+        def _():
+            act(self.hand_over)
+
+        @pl.when(self.time != 0)
+        def _():
+            for cut in IN_TIME:
+                act(self.remote[cut])
 
     def start(self, cuts):
+        if self.relayed:
+            self.over_time(lambda copy: copy.start())
+            cuts = [cut for cut in cuts if not cut[0]]
         for cut in cuts:
             if cut == STAYS:
                 pl.when(self.away)(self.remote[cut].start)
@@ -137,9 +193,24 @@
             else:
                 self.remote[cut].start()
 
+    def pass_on(self):
+        @pl.when(self.time == RELAY)
+        def _():
+            self.hand_over.wait_recv()
+            for copy in self.onward:
+                copy.start()
+
+    def wait_passed_on(self):
+        @pl.when(self.time == RELAY)
+        def _():
+            for copy in self.onward:
+                copy.wait_send()
+
     def wait_sent(self):
+        self.over_time(lambda copy: copy.wait_send())
         for cut in AWAY:
-            self.remote[cut].wait_send()
+            if not cut[0]:
+                self.remote[cut].wait_send()
         pl.when(self.away)(self.remote[STAYS].wait_send)
 
     def wait_received(self):
@@ -260,6 +331,8 @@
         clip_in,
         goal_in,
         back_out,
+        clip_relay,
+        goal_relay,
         slab_ref,
         spread_ref,
         skew_ref,
@@ -279,6 +352,8 @@
         send_sems,
         recv_sems,
         local_sems,
+        relay_sems,
+        onward_sems,
     ) = refs[2 * count + 3 :]
 
     loads = {}
@@ -288,21 +363,29 @@
         loads[name] = (pltpu.make_async_copy(sources[i], held[i], load_sems.at[i]), held[i])
         loads[name][0].start()
 
-    away = crosses(position()[0])
+    time_pos, row_pos, col_pos = position()
+    away = crosses(time_pos)
     barrier = pltpu.get_barrier_semaphore()
     for cut in AWAY:
-        pl.semaphore_signal(barrier, inc=1, device_id=source(cut), device_id_type=MESH)
+        pl.semaphore_signal(barrier, inc=1, device_id=sender(cut), device_id_type=MESH)
 
     @pl.when(away)
     def _():
         pl.semaphore_signal(barrier, inc=1, device_id=source(STAYS), device_id_type=MESH)
 
-    clip, goal, back = (
-        Exchange(src, dst, send_sems.at[k], recv_sems.at[k], local_sems.at[k], k < 2)
-        for k, (src, dst) in enumerate(
-            ((clip_ref, clip_in), (goal_ref, goal_in), (back_out, out_ref))
-        )
-    )
+    @pl.when(time_pos == RELAY)
+    def _():
+        first_block = device(0, row_pos, col_pos)
+        pl.semaphore_signal(barrier, inc=1, device_id=first_block, device_id_type=MESH)
+
+    sems = [
+        (send_sems.at[k], recv_sems.at[k], local_sems.at[k], relay_sems.at[k], onward_sems.at[k])
+        for k in range(2)
+    ]
+    clip = Exchange(clip_ref, clip_in, sems[0], True, clip_relay)
+    goal = Exchange(goal_ref, goal_in, sems[1], True, goal_relay)
+    back_sems = (send_sems.at[2], recv_sems.at[2], local_sems.at[2])
+    back = Exchange(back_out, out_ref, back_sems, False)
     for i in range(count):
         load(i)
 
@@ -311,12 +394,17 @@
         copy.wait()
         return ref[...]
 
-    pl.semaphore_wait(barrier, jnp.where(away, len(CUTS), len(AWAY)))
+    targets = jnp.where(away, len(CUTS), len(AWAY))
+    targets = targets + jnp.where(time_pos == RELAY, len(IN_TIME), 0)
+    targets = targets - jnp.where(time_pos == 0, len(IN_TIME) - 1, 0)
+    pl.semaphore_wait(barrier, targets)
     clip.start(CUTS)
+    clip.pass_on()
     spread_bias(operand("table"), slab_ref, spread_ref)
     clip.wait_sent()
     goal.start(CUTS)
     fill_bias(spread_ref, skew_ref, bias_ref)
+    goal.pass_on()
 
     lane = iota((1, CHAN), 1)
     spot = lane % HEAD
@@ -472,6 +560,8 @@
         back.start([cut for cut in CUTS if cut[1] == group])
     back.wait_received()
     goal.wait_sent()
+    clip.wait_passed_on()
+    goal.wait_passed_on()
     back.wait_sent()
 
 
@@ -521,6 +611,7 @@
         scratch_shapes=[pltpu.VMEM(x.shape, x.dtype) for x in operands]
         + [pltpu.SemaphoreType.DMA((len(operands),))]
         + [pltpu.VMEM((WH, WW, 2, ST, CHAN), BF16)] * 3
+        + [pltpu.VMEM((WH, WW, ST, CHAN), BF16)] * 2
         + [
             pltpu.VMEM((HEADS * (2 * WT - 1), plane), F32),
             pltpu.VMEM((2 * WH - 1, HEADS * (2 * WT - 1), 128), F32),
@@ -541,6 +632,8 @@
             pltpu.SemaphoreType.DMA((3, len(CUTS))),
             pltpu.SemaphoreType.DMA((3, len(CUTS))),
             pltpu.SemaphoreType.DMA((3,)),
+            pltpu.SemaphoreType.DMA((2, 2)),
+            pltpu.SemaphoreType.DMA((2, len(IN_TIME))),
         ],
         compiler_params=pltpu.CompilerParams(
             collective_id=0, has_side_effects=True, vmem_limit_bytes=40 * 1024 * 1024

time: 29.2 us -> 27.6 us (0.945)
  Pallas kernels: 28.5 us -> 26.8 us
    pallas_call x1, Pallas kernels: 28.5 us -> 26.8 us  [shards(): pl.pallas_call(kernel, out_shape=pltpu.VMEM((WH, WW, 2, ST, CHAN), BF16),...]
where the time goes in v6:
time: 27.6 us; the launch traced here: 27.5 us
  Pallas kernels  26.8 us (97%)
  local copies, waits for them, and re-layouts  0.64 us (2%)
    pallas_call x1, Pallas kernels, shards(): pl.pallas_call(kernel, out_shape=pltpu.VMEM((WH, WW, 2, ST, CHAN), BF16),...  26.8 us
    unnamed x1, local copies, waits for them, and re-layouts  0.64 us

profile of v6, /device:TPU:32, one launch (start us, length us, event | category | flops | bytes accessed | tf_op | source)
XLA Modules:
  0.0 27.5 jit_solution(5810650708727246514)
XLA Ops:
  0.0 26.8 %window_block.1 = bf16[7,7,2,4,128]{4,3,2,1,0:T(4,128)(2,1)S(1)} custom-call(bf16[7,7,2,4,128]{4,3,2,1,0:T(4,128)(2,1)} %bitcast.19, bf16[7,7,2,4,128]{4,3,2,1,0:T(4,128)(2,1)} %bitcast.20, f32[4,2535]{1,0:T(4,128)} %bitcast.21, f32[1,128]{1,0:T(1,128)} %bitcast.24, f32[1,128]{1,0:T(1,128)} %bitcast.25, bf16[128,384]{1,0:T(8,128)(2,1)} %refs_5_.1, ...), custom_call_target="tpu_custom_call" | custom-call | tf_op jit(solution)/shard_map/window_block/pallas_call | solution.py:606
  26.8 0.6 %copy.17 = bf16[8,1,7,7,128]{4,0,3,2,1:T(8,128)(2,1)} copy(bf16[8,1,7,7,128]{4,0,3,2,1:T(8,128)(2,1)S(1)} %bitcast.18) | data formatting | bytes 200704

commit v7 on v6

--- a/solution.py
+++ b/solution.py
@@ -228,6 +228,7 @@
 def spread_bias(table, slab_ref, spread_ref):
     time_span, row_span, col_span = 2 * WT - 1, 2 * WH - 1, 2 * WW - 1
     plane = row_span * col_span
+    slab_ref[HEADS * time_span :, :] = jnp.zeros((HEADS, plane), F32)
     for d in range(time_span):
         slab_ref[HEADS * d : HEADS * (d + 1), :] = table[:, d * plane : (d + 1) * plane]
     slabs = slab_ref[...] * LOG2E
@@ -239,25 +240,28 @@
     slot = lanes % 128 // WT
     wanted = jnp.where(slot < col_span, lanes // 128 * col_span + (col_span - 1) - slot, -1)
     pick = (iota((plane, row_span * 128), 0) == wanted).astype(F32).astype(BF16)
-    spread = (dot(low, pick) + dot(middle, pick)) + dot(high, pick)
+    spread = dot(jnp.concatenate([low, middle, high], axis=0), pick)
+    count = slabs.shape[0]
+    spread = (spread[:count] + spread[count : 2 * count]) + spread[2 * count :]
     for p in range(row_span):
         spread_ref[p] = spread[:, p * 128 : (p + 1) * 128]
 
 
-def fill_bias(spread_ref, skew_ref, bias_ref):
+def fill_bias(heads, spread_ref, skew_ref, bias_ref):
     row_span = 2 * WH - 1
     lane_time = iota((WT, 128), 1) % WT
     first = iota((WT, 128), 1) < 64
 
-    def fill_head(h, _):
+    for h in heads:
         for p in range(row_span):
             skewed = None
             for a in range(WT):
                 rows = spread_ref[p, pl.ds((WT - 1 - a) * HEADS + h, WT, stride=HEADS), :]
                 skewed = rows if skewed is None else jnp.where(lane_time == a, rows, skewed)
-            skew_ref[p] = skewed
+            skew_ref[h, p] = skewed
+    for h in heads:
         for d in range(row_span):
-            one, two = skew_ref[d], skew_ref[max(d - 1, 0)]
+            one, two = skew_ref[h, d], skew_ref[h, max(d - 1, 0)]
             for c in range(WW):
                 shift = WT * (WW - 1 - c)
                 bias_ref[h, d * WW + c] = jnp.where(
@@ -265,9 +269,6 @@
                     one if shift == 0 else pltpu.roll(one, 128 - shift, 1),
                     pltpu.roll(two, 64 - shift, 1),
                 )
-        return _
-
-    lax.fori_loop(0, HEADS, fill_head, 0)
 
 
 def gelu_parts(pre_act):
@@ -401,9 +402,10 @@
     clip.start(CUTS)
     clip.pass_on()
     spread_bias(operand("table"), slab_ref, spread_ref)
+    fill_bias((0, 1), spread_ref, skew_ref, bias_ref)
     clip.wait_sent()
     goal.start(CUTS)
-    fill_bias(spread_ref, skew_ref, bias_ref)
+    fill_bias((2, 3), spread_ref, skew_ref, bias_ref)
     goal.pass_on()
 
     lane = iota((1, CHAN), 1)
@@ -613,9 +615,9 @@
         + [pltpu.VMEM((WH, WW, 2, ST, CHAN), BF16)] * 3
         + [pltpu.VMEM((WH, WW, ST, CHAN), BF16)] * 2
         + [
-            pltpu.VMEM((HEADS * (2 * WT - 1), plane), F32),
-            pltpu.VMEM((2 * WH - 1, HEADS * (2 * WT - 1), 128), F32),
-            pltpu.VMEM((2 * WH - 1, WT, 128), F32),
+            pltpu.VMEM((HEADS * 2 * WT, plane), F32),
+            pltpu.VMEM((2 * WH - 1, HEADS * 2 * WT, 128), F32),
+            pltpu.VMEM((HEADS, 2 * WH - 1, WT, 128), F32),
             pltpu.VMEM((HEADS, (2 * WH - 1) * WW + 1, WT, 128), F32),
             pltpu.VMEM((HEADS, ROWS, KEYS), F32),
             pltpu.VMEM((HEADS, ROWS, KEYS), BF16),

time: 27.6 us -> 27.6 us (level)
  no operation moved by 1% of the time
where the time goes in v7:
time: 27.6 us; the launch traced here: 27.5 us
  Pallas kernels  26.8 us (97%)
  local copies, waits for them, and re-layouts  0.64 us (2%)
    pallas_call x1, Pallas kernels, shards(): pl.pallas_call(kernel, out_shape=pltpu.VMEM((WH, WW, 2, ST, CHAN), BF16),...  26.8 us
    unnamed x1, local copies, waits for them, and re-layouts  0.64 us

profile of v7, /device:TPU:32, one launch (start us, length us, event | category | flops | bytes accessed | tf_op | source)
XLA Modules:
  0.0 27.5 jit_solution(10159750476752358852)
XLA Ops:
  0.0 26.8 %window_block.1 = bf16[7,7,2,4,128]{4,3,2,1,0:T(4,128)(2,1)S(1)} custom-call(bf16[7,7,2,4,128]{4,3,2,1,0:T(4,128)(2,1)} %bitcast.19, bf16[7,7,2,4,128]{4,3,2,1,0:T(4,128)(2,1)} %bitcast.20, f32[4,2535]{1,0:T(4,128)} %bitcast.21, f32[1,128]{1,0:T(1,128)} %bitcast.24, f32[1,128]{1,0:T(1,128)} %bitcast.25, bf16[128,384]{1,0:T(8,128)(2,1)} %refs_5_.1, ...), custom_call_target="tpu_custom_call" | custom-call | tf_op jit(solution)/shard_map/window_block/pallas_call | solution.py:608
  26.8 0.6 %copy.17 = bf16[8,1,7,7,128]{4,0,3,2,1:T(8,128)(2,1)} copy(bf16[8,1,7,7,128]{4,0,3,2,1:T(8,128)(2,1)S(1)} %bitcast.18) | data formatting | bytes 200704

commit v8 on v7

--- a/solution.py
+++ b/solution.py
@@ -41,8 +41,8 @@
 
 
 CUTS = sorted(itertools.product(range(2), range(2), range(2)), reverse=True)
-AWAY, STAYS = CUTS[:-1], CUTS[-1]
-IN_TIME = [cut for cut in AWAY if cut[0]]
+IN_TIME = [cut for cut in CUTS if cut[0]]
+IN_PLACE = [cut for cut in CUTS if not cut[0]]
 RELAY = TM // 2 - 1
 HALVES = (slice(0, 192), slice(192, TOK))
 QUARTERS = (slice(0, 96), slice(96, 192), slice(192, 288), slice(288, TOK))
@@ -92,8 +92,22 @@
     return time % (TM // 2) == TM // 2 - 1
 
 
-def swapped(time, row):
-    return jnp.where(crosses(time), (row + TROWS // 2) % TROWS, row)
+def spread_out(window):
+    return jnp.where(window == 0, 0, jnp.where(window == 3, 1, window + 1))
+
+
+def gathered(place):
+    return jnp.where(place == 0, 0, jnp.where(place == 1, 3, place - 1))
+
+
+def row_place(time, window):
+    return jnp.where(crosses(time), (window + TROWS // 2) % TROWS, spread_out(window))
+
+
+def window_position():
+    time, row, col = position()
+    window_row = jnp.where(crosses(time), (row + TROWS // 2) % TROWS, gathered(row))
+    return time, window_row, gathered(col)
 
 
 def device(time, row, col):
@@ -103,14 +117,29 @@
 def target(cut):
     time, row, col = position()
     time = (time + TM - cut[0]) % TM
-    row = swapped(time, (row + TROWS - cut[1]) % TROWS)
-    return device(time, row, (col + TCOLS - cut[2]) % TCOLS)
+    row = row_place(time, (row + TROWS - cut[1]) % TROWS)
+    return device(time, row, spread_out((col + TCOLS - cut[2]) % TCOLS))
 
 
 def source(cut):
-    time, row, col = position()
-    row = swapped(time, row)
+    time, row, col = window_position()
     return device((time + cut[0]) % TM, (row + cut[1]) % TROWS, (col + cut[2]) % TCOLS)
+
+
+def stays(cut):
+    return source(cut)["tile"] == lax.axis_index("tile")
+
+
+def where_it_lies(cut, local, remote):
+    if cut[0]:
+        remote()
+    else:
+        pl.when(stays(cut))(local)
+        pl.when(jnp.logical_not(stays(cut)))(remote)
+
+
+def nothing():
+    pass
 
 
 def sender(cut):
@@ -122,9 +151,8 @@
 
 class Exchange:
     def __init__(self, src, dst, sems, to_window, relay=None):
-        send_sems, recv_sems, local_sem = sems[:3]
+        send_sems, recv_sems, local_sems = sems[:3]
         self.time, row, col = position()
-        self.away = crosses(self.time)
         self.remote = {
             cut: pltpu.make_async_remote_copy(
                 src_ref=src.at[box(cut, not to_window)],
@@ -136,9 +164,13 @@
             )
             for i, cut in enumerate(CUTS)
         }
-        self.local = pltpu.make_async_copy(
-            src.at[box(STAYS, not to_window)], dst.at[box(STAYS, to_window)], local_sem
-        )
+        self.local = {
+            cut: pltpu.make_async_copy(
+                src.at[box(cut, not to_window)], dst.at[box(cut, to_window)], local_sems.at[i]
+            )
+            for i, cut in enumerate(CUTS)
+            if not cut[0]
+        }
         self.relayed = to_window
         if not to_window:
             return
@@ -159,8 +191,8 @@
                 recv_sem=recv_sems.at[CUTS.index(cut)],
                 device_id=device(
                     TM - 1,
-                    swapped(TM - 1, (row + TROWS - cut[1]) % TROWS),
-                    (col + TCOLS - cut[2]) % TCOLS,
+                    row_place(TM - 1, (row + TROWS - cut[1]) % TROWS),
+                    spread_out((col + TCOLS - cut[2]) % TCOLS),
                 ),
                 device_id_type=MESH,
             )
@@ -187,11 +219,10 @@
             self.over_time(lambda copy: copy.start())
             cuts = [cut for cut in cuts if not cut[0]]
         for cut in cuts:
-            if cut == STAYS:
-                pl.when(self.away)(self.remote[cut].start)
-                pl.when(jnp.logical_not(self.away))(self.local.start)
+            if cut[0]:
+                self.remote[cut].start()
             else:
-                self.remote[cut].start()
+                where_it_lies(cut, self.local[cut].start, self.remote[cut].start)
 
     def pass_on(self):
         @pl.when(self.time == RELAY)
@@ -208,16 +239,14 @@
 
     def wait_sent(self):
         self.over_time(lambda copy: copy.wait_send())
-        for cut in AWAY:
-            if not cut[0]:
-                self.remote[cut].wait_send()
-        pl.when(self.away)(self.remote[STAYS].wait_send)
+        for cut in IN_PLACE:
+            where_it_lies(cut, nothing, self.remote[cut].wait_send)
 
     def wait_received(self):
-        for cut in AWAY:
+        for cut in IN_TIME:
             self.remote[cut].wait_recv()
-        pl.when(self.away)(self.remote[STAYS].wait_recv)
-        pl.when(jnp.logical_not(self.away))(self.local.wait)
+        for cut in IN_PLACE:
+            where_it_lies(cut, self.local[cut].wait, self.remote[cut].wait_recv)
 
 
 def joined(halves):
@@ -283,10 +312,10 @@
 
 
 def region_classes(row, col, time):
-    time_pos, row_pos, col_pos = position()
-    last_time = time_pos == TM - 1
-    last_row = swapped(time_pos, row_pos) == TROWS - 1
-    last_col = col_pos == TCOLS - 1
+    window_time, window_row, window_col = window_position()
+    last_time = window_time == TM - 1
+    last_row = window_row == TROWS - 1
+    last_col = window_col == TCOLS - 1
     return (
         jnp.where(time >= ST, jnp.where(last_time, 4, 0), 0)
         + jnp.where(row >= WH - SH, jnp.where(last_row, 2, 0), 0)
@@ -365,14 +394,13 @@
         loads[name][0].start()
 
     time_pos, row_pos, col_pos = position()
-    away = crosses(time_pos)
     barrier = pltpu.get_barrier_semaphore()
-    for cut in AWAY:
+
+    def greet(cut):
         pl.semaphore_signal(barrier, inc=1, device_id=sender(cut), device_id_type=MESH)
 
-    @pl.when(away)
-    def _():
-        pl.semaphore_signal(barrier, inc=1, device_id=source(STAYS), device_id_type=MESH)
+    for cut in CUTS:
+        where_it_lies(cut, nothing, lambda cut=cut: greet(cut))
 
     @pl.when(time_pos == RELAY)
     def _():
@@ -395,7 +423,9 @@
         copy.wait()
         return ref[...]
 
-    targets = jnp.where(away, len(CUTS), len(AWAY))
+    targets = len(CUTS)
+    for cut in IN_PLACE:
+        targets = targets - jnp.where(stays(cut), 1, 0)
     targets = targets + jnp.where(time_pos == RELAY, len(IN_TIME), 0)
     targets = targets - jnp.where(time_pos == 0, len(IN_TIME) - 1, 0)
     pl.semaphore_wait(barrier, targets)
@@ -633,7 +663,7 @@
             pltpu.VMEM((TOK, CHAN), F32),
             pltpu.SemaphoreType.DMA((3, len(CUTS))),
             pltpu.SemaphoreType.DMA((3, len(CUTS))),
-            pltpu.SemaphoreType.DMA((3,)),
+            pltpu.SemaphoreType.DMA((3, len(CUTS))),
             pltpu.SemaphoreType.DMA((2, 2)),
             pltpu.SemaphoreType.DMA((2, len(IN_TIME))),
         ],

time: 27.6 us -> 27 us (0.978)
  Pallas kernels: 26.8 us -> 26.2 us
    pallas_call x1, Pallas kernels: 26.8 us -> 26.2 us  [shards(): pl.pallas_call(kernel, out_shape=pltpu.VMEM((WH, WW, 2, ST, CHAN), BF16),...]
where the time goes in v8:
time: 27 us; the launch traced here: 26.9 us
  Pallas kernels  26.2 us (97%)
  local copies, waits for them, and re-layouts  0.64 us (2%)
    pallas_call x1, Pallas kernels, shards(): pl.pallas_call(kernel, out_shape=pltpu.VMEM((WH, WW, 2, ST, CHAN), BF16),...  26.2 us
    unnamed x1, local copies, waits for them, and re-layouts  0.64 us

profile of v8, /device:TPU:32, one launch (start us, length us, event | category | flops | bytes accessed | tf_op | source)
XLA Modules:
  0.0 26.9 jit_solution(7982026170505265917)
XLA Ops:
  0.0 26.2 %window_block.1 = bf16[7,7,2,4,128]{4,3,2,1,0:T(4,128)(2,1)S(1)} custom-call(bf16[7,7,2,4,128]{4,3,2,1,0:T(4,128)(2,1)} %bitcast.19, bf16[7,7,2,4,128]{4,3,2,1,0:T(4,128)(2,1)} %bitcast.20, f32[4,2535]{1,0:T(4,128)} %bitcast.21, f32[1,128]{1,0:T(1,128)} %bitcast.24, f32[1,128]{1,0:T(1,128)} %bitcast.25, bf16[128,384]{1,0:T(8,128)(2,1)} %refs_5_.1, ...), custom_call_target="tpu_custom_call" | custom-call | tf_op jit(solution)/shard_map/window_block/pallas_call | solution.py:638
  26.2 0.6 %copy.17 = bf16[8,1,7,7,128]{4,0,3,2,1:T(8,128)(2,1)} copy(bf16[8,1,7,7,128]{4,0,3,2,1:T(8,128)(2,1)S(1)} %bitcast.18) | data formatting | bytes 200704

commit v9 on v8

--- a/solution.py
+++ b/solution.py
@@ -145,7 +145,9 @@
 def sender(cut):
     where = source(cut)
     if cut[0]:
-        where["tm"] = jnp.where(position()[0] == TM - 1, RELAY, where["tm"])
+        time, _, col = position()
+        relay = device(RELAY, where["tile"] // TCOLS, col)
+        where = {axis: jnp.where(time == TM - 1, relay[axis], where[axis]) for axis in where}
     return where
 
 
@@ -175,25 +177,24 @@
         if not to_window:
             return
         relay_sems, onward_sems = sems[3:]
-        self.hand_over = pltpu.make_async_remote_copy(
-            src_ref=src.at[:, :, 0],
-            dst_ref=relay,
-            send_sem=relay_sems.at[0],
-            recv_sem=relay_sems.at[1],
-            device_id=device(RELAY, row, col),
-            device_id_type=MESH,
-        )
+        self.hand_over = [
+            pltpu.make_async_remote_copy(
+                src_ref=src.at[:, box((1, 0, ec), False)[1], 0],
+                dst_ref=relay.at[:, box((1, 0, ec), True)[1]],
+                send_sem=relay_sems.at[0, ec],
+                recv_sem=relay_sems.at[1, ec],
+                device_id=device(RELAY, row, spread_out((col + TCOLS - ec) % TCOLS)),
+                device_id_type=MESH,
+            )
+            for ec in range(2)
+        ]
         self.onward = [
             pltpu.make_async_remote_copy(
-                src_ref=relay.at[box(cut, False)[:2]],
+                src_ref=relay.at[box(cut, False)[0], box(cut, True)[1]],
                 dst_ref=dst.at[box(cut, True)],
                 send_sem=onward_sems.at[i],
                 recv_sem=recv_sems.at[CUTS.index(cut)],
-                device_id=device(
-                    TM - 1,
-                    row_place(TM - 1, (row + TROWS - cut[1]) % TROWS),
-                    spread_out((col + TCOLS - cut[2]) % TCOLS),
-                ),
+                device_id=device(TM - 1, row_place(TM - 1, (row + TROWS - cut[1]) % TROWS), col),
                 device_id_type=MESH,
             )
             for i, cut in enumerate(IN_TIME)
@@ -207,7 +208,8 @@
 
         @pl.when(self.time == 0)
         def _():
-            act(self.hand_over)
+            for copy in self.hand_over:
+                act(copy)
 
         @pl.when(self.time != 0)
         def _():
@@ -227,7 +229,8 @@
     def pass_on(self):
         @pl.when(self.time == RELAY)
         def _():
-            self.hand_over.wait_recv()
+            for copy in self.hand_over:
+                copy.wait_recv()
             for copy in self.onward:
                 copy.start()
 
@@ -404,8 +407,9 @@
 
     @pl.when(time_pos == RELAY)
     def _():
-        first_block = device(0, row_pos, col_pos)
-        pl.semaphore_signal(barrier, inc=1, device_id=first_block, device_id_type=MESH)
+        for ec in range(2):
+            first_block = device(0, row_pos, (gathered(col_pos) + ec) % TCOLS)
+            pl.semaphore_signal(barrier, inc=1, device_id=first_block, device_id_type=MESH)
 
     sems = [
         (send_sems.at[k], recv_sems.at[k], local_sems.at[k], relay_sems.at[k], onward_sems.at[k])
@@ -427,10 +431,10 @@
     for cut in IN_PLACE:
         targets = targets - jnp.where(stays(cut), 1, 0)
     targets = targets + jnp.where(time_pos == RELAY, len(IN_TIME), 0)
-    targets = targets - jnp.where(time_pos == 0, len(IN_TIME) - 1, 0)
+    targets = targets - jnp.where(time_pos == 0, len(IN_TIME) - 2, 0)
     pl.semaphore_wait(barrier, targets)
+    clip.pass_on()
     clip.start(CUTS)
-    clip.pass_on()
     spread_bias(operand("table"), slab_ref, spread_ref)
     fill_bias((0, 1), spread_ref, skew_ref, bias_ref)
     clip.wait_sent()
@@ -664,7 +668,7 @@
             pltpu.SemaphoreType.DMA((3, len(CUTS))),
             pltpu.SemaphoreType.DMA((3, len(CUTS))),
             pltpu.SemaphoreType.DMA((3, len(CUTS))),
-            pltpu.SemaphoreType.DMA((2, 2)),
+            pltpu.SemaphoreType.DMA((2, 2, 2)),
             pltpu.SemaphoreType.DMA((2, len(IN_TIME))),
         ],
         compiler_params=pltpu.CompilerParams(

time: 27 us -> 28.4 us (1.052)
  the two profiles are of different devices: /device:TPU:32 before, /device:TPU:6 now
where the time goes in v9:
time: 28.4 us
  Pallas kernels  27.7 us (98%)
  local copies, waits for them, and re-layouts  0.64 us (2%)
    pallas_call x1, Pallas kernels, shards(): pl.pallas_call(kernel, out_shape=pltpu.VMEM((WH, WW, 2, ST, CHAN), BF16),...  27.7 us
    unnamed x1, local copies, waits for them, and re-layouts  0.64 us

profile of v9, /device:TPU:6, one launch (start us, length us, event | category | flops | bytes accessed | tf_op | source)
XLA Modules:
  0.0 28.4 jit_solution(14811295317980124491)
XLA Ops:
  0.0 27.7 %window_block.1 = bf16[7,7,2,4,128]{4,3,2,1,0:T(4,128)(2,1)S(1)} custom-call(bf16[7,7,2,4,128]{4,3,2,1,0:T(4,128)(2,1)} %bitcast.19, bf16[7,7,2,4,128]{4,3,2,1,0:T(4,128)(2,1)} %bitcast.20, f32[4,2535]{1,0:T(4,128)} %bitcast.21, f32[1,128]{1,0:T(1,128)} %bitcast.24, f32[1,128]{1,0:T(1,128)} %bitcast.25, bf16[128,384]{1,0:T(8,128)(2,1)} %refs_5_.1, ...), custom_call_target="tpu_custom_call" | custom-call | tf_op jit(solution)/shard_map/window_block/pallas_call | solution.py:642
  27.7 0.6 %copy.17 = bf16[8,1,7,7,128]{4,0,3,2,1:T(8,128)(2,1)} copy(bf16[8,1,7,7,128]{4,0,3,2,1:T(8,128)(2,1)S(1)} %bitcast.18) | data formatting | bytes 200704

commit v10 on v9

--- a/solution.py
+++ b/solution.py
@@ -433,8 +433,8 @@
     targets = targets + jnp.where(time_pos == RELAY, len(IN_TIME), 0)
     targets = targets - jnp.where(time_pos == 0, len(IN_TIME) - 2, 0)
     pl.semaphore_wait(barrier, targets)
+    clip.start(CUTS)
     clip.pass_on()
-    clip.start(CUTS)
     spread_bias(operand("table"), slab_ref, spread_ref)
     fill_bias((0, 1), spread_ref, skew_ref, bias_ref)
     clip.wait_sent()

time: 28.4 us -> 28.5 us (level)
  no operation moved by 1% of the time
where the time goes in v10:
time: 28.5 us; the launch traced here: 28.4 us
  Pallas kernels  27.8 us (98%)
  local copies, waits for them, and re-layouts  0.64 us (2%)
    pallas_call x1, Pallas kernels, shards(): pl.pallas_call(kernel, out_shape=pltpu.VMEM((WH, WW, 2, ST, CHAN), BF16),...  27.8 us
    unnamed x1, local copies, waits for them, and re-layouts  0.64 us

profile of v10, /device:TPU:6, one launch (start us, length us, event | category | flops | bytes accessed | tf_op | source)
XLA Modules:
  0.0 28.4 jit_solution(9303194362555941551)
XLA Ops:
  0.0 27.8 %window_block.1 = bf16[7,7,2,4,128]{4,3,2,1,0:T(4,128)(2,1)S(1)} custom-call(bf16[7,7,2,4,128]{4,3,2,1,0:T(4,128)(2,1)} %bitcast.19, bf16[7,7,2,4,128]{4,3,2,1,0:T(4,128)(2,1)} %bitcast.20, f32[4,2535]{1,0:T(4,128)} %bitcast.21, f32[1,128]{1,0:T(1,128)} %bitcast.24, f32[1,128]{1,0:T(1,128)} %bitcast.25, bf16[128,384]{1,0:T(8,128)(2,1)} %refs_5_.1, ...), custom_call_target="tpu_custom_call" | custom-call | tf_op jit(solution)/shard_map/window_block/pallas_call | solution.py:642
  27.8 0.6 %copy.17 = bf16[8,1,7,7,128]{4,0,3,2,1:T(8,128)(2,1)} copy(bf16[8,1,7,7,128]{4,0,3,2,1:T(8,128)(2,1)S(1)} %bitcast.18) | data formatting | bytes 200704
